TPU v7x, 128 devices: a whole 4x4x4 slice. The times are simulated.
128 devices in a mesh: gx: 16 (over z, y), gy: 8 (over x, core).
Axes of the slice: x: 4, y: 4, z: 4, core: 2. Of those that a mesh axis runs over, the one named last changes fastest.
Arguments:
- template: bfloat16 [512, 256, 256], P('gx', 'gy'), may hold values from -6 to 6
- target_image: bfloat16 [512, 256, 256], P('gx', 'gy'), may hold values from -6 to 6
- velocity: float32 [3, 512, 256, 256], P(None, 'gx', 'gy'), may hold values from -6 to 6
- operators: bfloat16 [64, 3, 32, 32], replicated, may hold values from -1 to 1
- route: int32 [2, 16, 8, 8, 1], P(None, 'gx', 'gy'), may hold values from 0 to 15; in each aligned block of 8 rows (0 to 7, 8 to 15, ..., all dimensions but the last counted through in order) at most 2 rows name the same one
- target_brick: int32 [2, 16, 8, 8], P(None, 'gx', 'gy'), may hold values from 0 to 7
- operator_index: int32 [2, 16, 8, 8], P(None, 'gx', 'gy'), may hold values from 0 to 63
Outputs:
- velocity_grad: float32 [3, 512, 256, 256], P(None, 'gx', 'gy')
- template_grad: bfloat16 [512, 256, 256], P('gx', 'gy')
Inputs may be any that keep to these rules, and one draw needn't show every extreme that they name: `route`: in every step, no device sends more than 2 of its bricks to one destination device, and some device sends exactly 2 to one; the destination keeps the second index.
All inputs are finite; a program needn't handle non-finite values.
Results may differ from a plain program's by a relative error of at most 0.0085.
Values may be sent and summed in bfloat16 or wider, within the bound.
A program may use at most 128 MiB of HBM per device.

v0:
```python
import jax
import jax.numpy as jnp
from jax import lax
from jax.sharding import PartitionSpec as P

STEPS = 2


HIGHEST_PRECISION = lax.Precision.HIGHEST


def extended(value, sides, width):
    for axis, dim in sides:
        size, length = (lax.axis_size(axis), value.shape[dim])
        up = [(i, (i + 1) % size) for i in range(size - 1)]
        down = [(j, i) for i, j in up]
        last = lax.slice_in_dim(value, length - width, length, axis=dim)
        initial = lax.slice_in_dim(value, 0, width, axis=dim)
        before = lax.ppermute(last, axis, up)
        after = lax.ppermute(initial, axis, down)
        value = jnp.concatenate([before, value, after], axis=dim)
    return value


def sixth_order(padded, axis_id):
    array_rank = padded.ndim

    def shifted(offset):
        slicer = []
        for dimension in range(array_rank):
            if dimension == array_rank - 3 + axis_id:
                slicer.append(slice(3 + offset, padded.shape[dimension] - 3 + offset))
            else:
                slicer.append(slice(3, padded.shape[dimension] - 3))
        return padded[tuple(slicer)]

    return (
        0.75 * (shifted(1) - shifted(-1))
        - 0.15 * (shifted(2) - shifted(-2))
        + (shifted(3) - shifted(-3)) / 60.0
    )


def pad_depth(field_in):
    widths = [(0, 0)] * (field_in.ndim - 1) + [(3, 3)]
    return jnp.pad(field_in, widths)


def split_bricks(field_in, edge_cells):
    cells_x, cells_y, depth_cells = field_in.shape
    brick_total = depth_cells // edge_cells
    shaped = field_in.reshape(cells_x, cells_y, brick_total, edge_cells).transpose(2, 0, 1, 3)
    return shaped.reshape(brick_total, cells_x, cells_y * edge_cells)


def join_bricks(bricks, edge_cells):
    brick_total = bricks.shape[0]
    shaped = bricks.reshape(brick_total, edge_cells, edge_cells, edge_cells).transpose(1, 2, 0, 3)
    return shaped.reshape(edge_cells, edge_cells, brick_total * edge_cells)


def lookup(operators, indices):
    tables = operators.shape[0]
    one_hot = (indices[:, None] == jnp.arange(tables, dtype=jnp.int32)[None, :]).astype(
        jnp.bfloat16
    )
    chosen = jnp.dot(one_hot, operators.reshape(tables, -1), preferred_element_type=jnp.float32)
    return chosen.astype(jnp.bfloat16).reshape((indices.shape[0],) + operators.shape[1:])


def apply_operator(matrices, bricks, flipped):
    brick_total, edge_cells = (bricks.shape[0], bricks.shape[1])
    square = edge_cells * edge_cells
    if flipped:
        forms_list = ["mar,max->mrx", "mbr,mby->mry", "mcr,mcz->mrz"]
    else:
        forms_list = ["mar,mxa->mrx", "mbr,myb->mry", "mcr,mzc->mrz"]
    section_one = jnp.einsum(
        forms_list[0], bricks, matrices[:, 0], preferred_element_type=jnp.float32
    )
    view_one = section_one.reshape(brick_total, edge_cells, square)
    section_two = jnp.einsum(
        forms_list[1], view_one, matrices[:, 1].astype(jnp.float32), precision=HIGHEST_PRECISION
    )
    view_two = section_two.reshape(brick_total, edge_cells, square)
    section_three = jnp.einsum(
        forms_list[2], view_two, matrices[:, 2].astype(jnp.float32), precision=HIGHEST_PRECISION
    )
    return section_three.reshape(brick_total, edge_cells, square)


def shards(template, target_image, velocity, operators, route, target_brick, operator_index):
    edge_cells = operators.shape[2]
    brick_total = template.shape[2] // edge_cells
    peer_count = lax.axis_size("gx")
    capacity = max(2, 2 * brick_total // peer_count)
    slot_count = peer_count * capacity
    volume = edge_cells * edge_cells * edge_cells
    brick_ids = jnp.arange(brick_total, dtype=jnp.int32)
    slot_ids = jnp.arange(slot_count, dtype=jnp.int32)
    states = [template]
    arrivals = []
    sendlists = []
    for section_id in range(STEPS):
        destination = route[section_id, 0, 0, :, 0]
        landing = target_brick[section_id, 0, 0]
        chosen_ops = operator_index[section_id, 0, 0]
        earlier = (destination[:, None] == destination[None, :]) & (
            brick_ids[:, None] > brick_ids[None, :]
        )
        position = destination * capacity + jnp.sum(earlier.astype(jnp.int32), axis=1)
        placing = slot_ids[:, None] == position[None, :]
        place_int = placing.astype(jnp.int32)
        place_half = placing.astype(jnp.bfloat16)
        slot_landing = (jnp.sum(place_int * (landing + 1)[None, :], axis=1) - 1).reshape(
            peer_count, capacity
        )
        bricks = split_bricks(states[-1], edge_cells)
        slot_ops = (jnp.sum(place_int * (chosen_ops + 1)[None, :], axis=1) - 1).reshape(
            peer_count, capacity
        )
        packed = jnp.dot(
            place_half, bricks.reshape(brick_total, volume), preferred_element_type=jnp.float32
        ).astype(jnp.bfloat16)
        received, got_landing, got_ops = (
            lax.all_to_all(
                packed.reshape(peer_count, capacity, volume),
                "gx",
                split_axis=0,
                concat_axis=0,
                tiled=True,
            ),
            lax.all_to_all(slot_landing, "gx", split_axis=0, concat_axis=0, tiled=True),
            lax.all_to_all(slot_ops, "gx", split_axis=0, concat_axis=0, tiled=True),
        )
        flat_ops = got_ops.reshape(slot_count)
        incoming = apply_operator(
            lookup(operators, flat_ops),
            received.reshape(slot_count, edge_cells, edge_cells * edge_cells),
            False,
        )
        incoming = incoming.astype(jnp.bfloat16).reshape(slot_count, volume)
        arrivals.append((got_landing.reshape(slot_count), flat_ops))
        sendlists.append((place_half, chosen_ops))
        gather_rows = (brick_ids[:, None] == got_landing.reshape(slot_count)[None, :]).astype(
            jnp.bfloat16
        )
        summed = jnp.dot(gather_rows, incoming, preferred_element_type=jnp.float32).astype(
            jnp.bfloat16
        )
        states.append(
            join_bricks(
                summed.reshape(brick_total, edge_cells, edge_cells * edge_cells), edge_cells
            )
        )
    adjoint = (states[-1].astype(jnp.float32) - target_image.astype(jnp.float32)).astype(
        jnp.bfloat16
    )
    accumulated = jnp.zeros((3,) + template.shape, jnp.float32)
    for section_id in reversed(range(STEPS)):
        rimmed = extended(states[section_id], (("gx", 0), ("gy", 1)), 3)
        padded = pad_depth(rimmed).astype(jnp.float32)
        weight = adjoint.astype(jnp.float32)
        accumulated = accumulated + jnp.stack(
            [weight * sixth_order(padded, axis_id) for axis_id in range(3)]
        )
        got_landing, got_ops = arrivals[section_id]
        place_half, chosen_ops = sendlists[section_id]
        later_bricks = split_bricks(adjoint, edge_cells).reshape(brick_total, volume)
        at_slots = (got_landing[:, None] == brick_ids[None, :]).astype(jnp.bfloat16)
        wanted = jnp.dot(at_slots, later_bricks, preferred_element_type=jnp.float32).astype(
            jnp.bfloat16
        )
        pulled = apply_operator(
            lookup(operators, got_ops),
            wanted.reshape(slot_count, edge_cells, edge_cells * edge_cells),
            True,
        )
        pulled = pulled.astype(jnp.bfloat16).reshape(peer_count, capacity, volume)
        returned = lax.all_to_all(pulled, "gx", split_axis=0, concat_axis=0, tiled=True)
        own_bricks = jnp.dot(
            place_half.T, returned.reshape(slot_count, volume), preferred_element_type=jnp.float32
        ).astype(jnp.bfloat16)
        adjoint = join_bricks(
            own_bricks.reshape(brick_total, edge_cells, edge_cells * edge_cells), edge_cells
        )
    velocity_rim = extended(velocity.astype(jnp.bfloat16), (("gx", 1), ("gy", 2)), 3).astype(
        velocity.dtype
    )
    velocity_pad = pad_depth(velocity_rim)
    divergence = (
        sixth_order(velocity_pad[0], 0)
        + sixth_order(velocity_pad[1], 1)
        + sixth_order(velocity_pad[2], 2)
    )
    divergence_rim = extended(divergence.astype(jnp.bfloat16), (("gx", 0), ("gy", 1)), 3).astype(
        divergence.dtype
    )
    divergence_pad = pad_depth(divergence_rim)
    regular = jnp.stack([sixth_order(divergence_pad, axis_id) for axis_id in range(3)])
    velocity_grad = accumulated / STEPS - 0.25 * regular
    return (velocity_grad, adjoint)


def solution(mesh):
    placed = (
        P("gx", "gy", None),
        P("gx", "gy", None),
        P(None, "gx", "gy", None),
        P(),
        P(None, "gx", "gy", None, None),
        P(None, "gx", "gy", None),
        P(None, "gx", "gy", None),
    )
    return jax.shard_map(
        shards,
        mesh=mesh,
        in_specs=placed,
        out_specs=(P(None, "gx", "gy", None), P("gx", "gy", None)),
        check_vma=False,
    )
```

profile of v0, /device:TPU:2, one launch (start us, length us, event | category | flops | bytes accessed | tf_op | source)
XLA Modules:
  0.0 630.0 jit_solution(15542549274062893130)
XLA Ops:
  3.8 8.0 %all-to-all-start.3 = ((s32[16,1,2]{2,1,0:T(1,128)}), s32[16,1,2]{2,1,0:T(1,128)S(1)}, u32[]{:S(2)}, u32[]{:S(2)}) async-start(s32[16,1,2]{2,1,0:T(1,128)} %bitcast.8), calls=%async_computation.3 | async-start | bytes 16384 | tf_op jit(solution)/shard_map/all_to_all | solution.py:134
  90.3 9.8 %fusion.93 = f32[32,1024,32]{2,1,0:T(8,128)} fusion(bf16[32,32,1024]{2,1,0:T(8,128)(2,1)} %reshape.232, bf16[32,3,32,32]{3,2,1,0:T(8,128)(2,1)S(1)} %reshape.234), kind=kOutput, calls=%fused_computation.177 | convolution fusion | flops 67108864 | bytes 6553600 | tf_op jit(solution)/shard_map/mar,mxa->mrx/dot_general | solution.py:78
  100.1 13.7 %reshape.235 = f32[32,32,1024]{2,1,0:T(8,128)} reshape(f32[32,1024,32]{2,1,0:T(8,128)} %fusion.93) | data formatting | bytes 8388608 | tf_op jit(solution)/shard_map/reshape | solution.py:81
  113.8 16.9 %fusion.95 = f32[32,1024,32]{2,1,0:T(8,128)} fusion(f32[32,32,1024]{2,1,0:T(8,128)} %reshape.235, bf16[32,3,32,32]{3,2,1,0:T(8,128)(2,1)S(1)} %reshape.234), kind=kOutput, calls=%fused_computation.179 | convolution fusion | flops 402653184 | bytes 8650752 | tf_op jit(solution)/shard_map/mbr,myb->mry/dot_general | solution.py:82
  130.7 13.7 %reshape.236 = f32[32,32,1024]{2,1,0:T(8,128)} reshape(f32[32,1024,32]{2,1,0:T(8,128)} %fusion.95) | data formatting | bytes 8388608 | tf_op jit(solution)/shard_map/reshape | solution.py:85
  150.1 7.8 %copy.104 = bf16[32,1024,32]{2,1,0:T(8,128)(2,1)} copy(bf16[32,1024,32]{1,2,0:T(8,128)(2,1)} %convolution_convert_fusion.13) | data formatting | bytes 4194304 | tf_op jit(solution)/shard_map/convert_element_type | solution.py:142
  157.9 11.5 %convert_element_type.147 = bf16[32,32768]{1,0:T(8,128)(2,1)} reshape(bf16[32,1024,32]{2,1,0:T(8,128)(2,1)} %copy.104) | data formatting | bytes 4194304 | tf_op jit(solution)/shard_map/convert_element_type | solution.py:142
  214.6 6.8 %fusion.2 = f32[3,38,38,262]{3,2,1,0:T(8,128)} fusion(bf16[3,38,3,256]{3,2,1,0:T(4,128)(2,1)} %collective-permute-done.11, bf16[3,38,3,256]{3,2,1,0:T(4,128)(2,1)} %collective-permute-done.10, bf16[3,3,32,256]{3,2,1,0:T(8,128)(2,1)S(1)} %collective-permute-done.9, bf16[3,32,32,256]{3,2,1,0:T(8,128)(2,1)S(1)} %convert_element_type.171, ...), kind=kLoop, calls=%fused_computation.19 | loop fusion | flops 20429712 | bytes 6757920 | tf_op jit(solution)/shard_map/jit(_pad)/pad | solution.py:46
  226.9 9.8 %fusion.97 = f32[32,1024,32]{2,1,0:T(8,128)} fusion(bf16[32,32,1024]{2,1,0:T(8,128)(2,1)} %reshape.238, bf16[32,3,32,32]{3,2,1,0:T(8,128)(2,1)} %reshape.239), kind=kOutput, calls=%fused_computation.181 | convolution fusion | flops 67108864 | bytes 6553600 | tf_op jit(solution)/shard_map/mar,mxa->mrx/dot_general | solution.py:78
  236.6 13.7 %reshape.240 = f32[32,32,1024]{2,1,0:T(8,128)} reshape(f32[32,1024,32]{2,1,0:T(8,128)} %fusion.97) | data formatting | bytes 8388608 | tf_op jit(solution)/shard_map/reshape | solution.py:81
  250.3 18.3 %fusion.99 = f32[32,1024,32]{2,1,0:T(8,128)} fusion(f32[32,32,1024]{2,1,0:T(8,128)} %reshape.240, bf16[32,3,32,32]{3,2,1,0:T(8,128)(2,1)} %reshape.239), kind=kOutput, calls=%fused_computation.183 | convolution fusion | flops 402653184 | bytes 8650752 | tf_op jit(solution)/shard_map/mbr,myb->mry/dot_general | solution.py:82
  268.6 13.8 %reshape.241 = f32[32,32,1024]{2,1,0:T(8,128)} reshape(f32[32,1024,32]{2,1,0:T(8,128)} %fusion.99) | data formatting | bytes 8388608 | tf_op jit(solution)/shard_map/reshape | solution.py:85
  288.1 7.8 %copy.111 = bf16[32,1024,32]{2,1,0:T(8,128)(2,1)} copy(bf16[32,1024,32]{1,2,0:T(8,128)(2,1)} %convolution_convert_fusion.12) | data formatting | bytes 4194304 | tf_op jit(solution)/shard_map/convert_element_type | solution.py:142
  295.9 11.3 %convert_element_type.152 = bf16[32,32768]{1,0:T(8,128)(2,1)} reshape(bf16[32,1024,32]{2,1,0:T(8,128)(2,1)} %copy.111) | data formatting | bytes 4194304 | tf_op jit(solution)/shard_map/convert_element_type | solution.py:142
  314.9 8.0 %copy.112 = f32[32,32,8,32]{3,2,1,0:T(8,128)} copy(f32[32,32,8,32]{3,1,0,2:T(8,128)} %bitcast.135) | data formatting | bytes 2097152 | tf_op jit(solution)/shard_map/convert_element_type | solution.py:156
  345.8 8.0 %fusion.96 = f32[32,1024,32]{2,1,0:T(8,128)} fusion(bf16[32,32,1024]{2,1,0:T(8,128)(2,1)S(1)} %bitcast.139, bf16[32,3,32,32]{3,2,1,0:T(8,128)(2,1)} %reshape.239), kind=kOutput, calls=%fused_computation.180 | convolution fusion | flops 67108864 | bytes 6553600 | tf_op jit(solution)/shard_map/mar,max->mrx/dot_general | solution.py:78
  353.8 13.7 %reshape.245 = f32[32,32,1024]{2,1,0:T(8,128)} reshape(f32[32,1024,32]{2,1,0:T(8,128)} %fusion.96) | data formatting | bytes 8388608 | tf_op jit(solution)/shard_map/reshape | solution.py:81
  367.5 18.7 %fusion.98 = f32[32,1024,32]{2,1,0:T(8,128)} fusion(f32[32,32,1024]{2,1,0:T(8,128)} %reshape.245, bf16[32,3,32,32]{3,2,1,0:T(8,128)(2,1)} %reshape.239), kind=kOutput, calls=%fused_computation.182 | convolution fusion | flops 402653184 | bytes 8650752 | tf_op jit(solution)/shard_map/mbr,mby->mry/dot_general | solution.py:82
  386.2 13.7 %reshape.246 = f32[32,32,1024]{2,1,0:T(8,128)} reshape(f32[32,1024,32]{2,1,0:T(8,128)} %fusion.98) | data formatting | bytes 8388608 | tf_op jit(solution)/shard_map/reshape | solution.py:85
  405.5 7.8 %copy.122 = bf16[32,1024,32]{2,1,0:T(8,128)(2,1)} copy(bf16[32,1024,32]{1,2,0:T(8,128)(2,1)} %convolution_convert_fusion.11) | data formatting | bytes 4194304 | tf_op jit(solution)/shard_map/convert_element_type | solution.py:179
  413.4 14.5 %convert_element_type.164 = bf16[16,2,32768]{2,1,0:T(2,128)(2,1)} reshape(bf16[32,1024,32]{2,1,0:T(8,128)(2,1)} %copy.122) | data formatting | bytes 4194304 | tf_op jit(solution)/shard_map/convert_element_type | solution.py:179
  427.8 8.3 %all-to-all-start.6 = ((bf16[16,2,32768]{2,1,0:T(2,128)(2,1)}), bf16[16,2,32768]{2,1,0:T(2,128)(2,1)}, u32[]{:S(2)}, u32[]{:S(2)}) async-start(bf16[16,2,32768]{2,1,0:T(2,128)(2,1)} %convert_element_type.164), calls=%async_computation.6 | async-start | bytes 4194304 | tf_op jit(solution)/shard_map/all_to_all | solution.py:180
  456.1 13.8 %collective-permute-done.13 = bf16[3,32,256]{2,1,0:T(8,128)(2,1)S(1)} collective-permute-done((bf16[3,32,256]{2,1,0:T(8,128)(2,1)S(1)}, bf16[3,32,256]{2,1,0:T(8,128)(2,1)S(1)}, u32[]{:S(2)}, u32[]{:S(2)}) %collective-permute-start.13) | collective-permute-done | bytes 49184 | tf_op jit(solution)/shard_map/ppermute | solution.py:20
  487.6 7.1 %fusion.92 = f32[32,1024,32]{2,1,0:T(8,128)} fusion(bf16[32,32,1024]{2,1,0:T(8,128)(2,1)S(1)} %bitcast.140, bf16[32,3,32,32]{3,2,1,0:T(8,128)(2,1)S(1)} %reshape.234), kind=kOutput, calls=%fused_computation.176 | convolution fusion | flops 67108864 | bytes 6553600 | tf_op jit(solution)/shard_map/mar,max->mrx/dot_general | solution.py:78
  494.7 13.7 %reshape.249 = f32[32,32,1024]{2,1,0:T(8,128)} reshape(f32[32,1024,32]{2,1,0:T(8,128)} %fusion.92) | data formatting | bytes 8388608 | tf_op jit(solution)/shard_map/reshape | solution.py:81
  508.4 16.9 %fusion.94 = f32[32,1024,32]{2,1,0:T(8,128)} fusion(f32[32,32,1024]{2,1,0:T(8,128)} %reshape.249, bf16[32,3,32,32]{3,2,1,0:T(8,128)(2,1)S(1)} %reshape.234), kind=kOutput, calls=%fused_computation.178 | convolution fusion | flops 402653184 | bytes 8650752 | tf_op jit(solution)/shard_map/mbr,mby->mry/dot_general | solution.py:82
  525.3 13.9 %reshape.250 = f32[32,32,1024]{2,1,0:T(8,128)} reshape(f32[32,1024,32]{2,1,0:T(8,128)} %fusion.94) | data formatting | bytes 8388608 | tf_op jit(solution)/shard_map/reshape | solution.py:85
  545.0 7.8 %copy.129 = bf16[32,1024,32]{2,1,0:T(8,128)(2,1)} copy(bf16[32,1024,32]{1,2,0:T(8,128)(2,1)} %convolution_convert_fusion.10) | data formatting | bytes 4194304 | tf_op jit(solution)/shard_map/convert_element_type | solution.py:179
  552.8 14.5 %convert_element_type.176 = bf16[16,2,32768]{2,1,0:T(2,128)(2,1)} reshape(bf16[32,1024,32]{2,1,0:T(8,128)(2,1)} %copy.129) | data formatting | bytes 4194304 | tf_op jit(solution)/shard_map/convert_element_type | solution.py:179
  567.3 6.8 %all-to-all-start.7 = ((bf16[16,2,32768]{2,1,0:T(2,128)(2,1)}), bf16[16,2,32768]{2,1,0:T(2,128)(2,1)}, u32[]{:S(2)}, u32[]{:S(2)}) async-start(bf16[16,2,32768]{2,1,0:T(2,128)(2,1)} %convert_element_type.176), calls=%async_computation.7 | async-start | bytes 4194304 | tf_op jit(solution)/shard_map/all_to_all | solution.py:180
  574.1 14.1 %fusion.34 = (f32[1,32,32,256]{3,2,1,0:T(8,128)}, f32[1,32,32,256]{3,2,1,0:T(8,128)}, f32[1,32,32,256]{3,2,1,0:T(8,128)}) fusion(f32[38,38,256]{2,1,0:T(8,128)} %maximum_convert_fusion), kind=kLoop, calls=%fused_computation.78 | loop fusion | flops 6291456 | bytes 17285120 | tf_op jit(solution)/shard_map/stack | solution.py:200
  595.8 8.0 %copy.123 = f32[32,32,8,32]{3,2,1,0:T(8,128)} copy(f32[32,32,8,32]{3,1,0,2:T(8,128)} %bitcast.136) | data formatting | bytes 2097152 | tf_op jit(solution)/shard_map/convert_element_type | solution.py:163
  (171 shorter events, 256.1 us)
Async XLA Ops:
  0.6 74.3 %copy-start = (bf16[64,3,32,32]{0,3,2,1:T(8,128)(2,1)S(1)}, bf16[64,3,32,32]{0,3,2,1:T(8,128)(2,1)}, u32[]{:S(2)}) copy-start(bf16[64,3,32,32]{0,3,2,1:T(8,128)(2,1)} %param.10) | copy-start | bytes 1179652
  2.3 23.0 %copy-start.16 = (s32[8]{0:T(128)}, s32[8]{0:T(128)S(1)}, u32[]{:S(2)}) copy-start(s32[8]{0:T(128)S(1)} %get-tuple-element.39) | copy-start | bytes 100
  2.3 43.0 %copy-start.14 = (s32[8]{0:T(128)}, s32[8]{0:T(128)S(1)}, u32[]{:S(2)}) copy-start(s32[8]{0:T(128)S(1)} %get-tuple-element.40) | copy-start | bytes 100
  3.8 15.5 %all-to-all-start.3 = ((s32[16,1,2]{2,1,0:T(1,128)}), s32[16,1,2]{2,1,0:T(1,128)S(1)}, u32[]{:S(2)}, u32[]{:S(2)}) async-start(s32[16,1,2]{2,1,0:T(1,128)} %bitcast.8), calls=%async_computation.3 | async-start | bytes 16384 | tf_op jit(solution)/shard_map/all_to_all | solution.py:134
  19.3 11.6 %all-to-all-start.1 = ((s32[16,1,2]{2,1,0:T(1,128)}), s32[16,1,2]{2,1,0:T(1,128)S(1)}, u32[]{:S(2)}, u32[]{:S(2)}) async-start(s32[16,1,2]{2,1,0:T(1,128)} %bitcast.5), calls=%async_computation.1 | async-start | bytes 16384 | tf_op jit(solution)/shard_map/all_to_all | solution.py:133
  30.9 10.9 %all-to-all-start.5 = ((s32[16,1,2]{2,1,0:T(1,128)}), s32[16,1,2]{2,1,0:T(1,128)S(1)}, u32[]{:S(2)}, u32[]{:S(2)}) async-start(s32[16,1,2]{2,1,0:T(1,128)} %bitcast.14), calls=%async_computation.5 | async-start | bytes 16384 | tf_op jit(solution)/shard_map/all_to_all | solution.py:134
  41.8 10.9 %all-to-all-start = ((s32[16,1,2]{2,1,0:T(1,128)}), s32[16,1,2]{2,1,0:T(1,128)S(1)}, u32[]{:S(2)}, u32[]{:S(2)}) async-start(s32[16,1,2]{2,1,0:T(1,128)} %bitcast.2), calls=%async_computation | async-start | bytes 16384 | tf_op jit(solution)/shard_map/all_to_all | solution.py:133
  48.7 8.5 %copy-start.13 = (bf16[32,32,256]{2,1,0:T(8,128)(2,1)S(1)}, bf16[32,32,256]{2,1,0:T(8,128)(2,1)}, u32[]{:S(2)}) copy-start(bf16[32,32,256]{2,1,0:T(8,128)(2,1)} %param.7) | copy-start | bytes 1572868
  52.8 32.9 %all-to-all-start.2 = ((bf16[16,2,32768]{2,1,0:T(2,128)(2,1)}), bf16[16,2,32768]{2,1,0:T(2,128)(2,1)}, u32[]{:S(2)}, u32[]{:S(2)}) async-start(bf16[16,2,32768]{2,1,0:T(2,128)(2,1)} %reshape.231), calls=%async_computation.2 | async-start | bytes 4194304 | tf_op jit(solution)/shard_map/all_to_all | solution.py:126
  57.9 21.6 %collective-permute-start.4 = (bf16[3,32,256]{2,1,0:T(8,128)(2,1)}, bf16[3,32,256]{2,1,0:T(8,128)(2,1)S(1)}, u32[]{:S(2)}, u32[]{:S(2)}) collective-permute-start(bf16[3,32,256]{2,1,0:T(8,128)(2,1)} %get-tuple-element.34), channel_id=1, source_target_pairs={{0,8},{8,16},{16,24},{24,32},{32,40},{40,48},{48,56},{56,64},{64,7... | collective-permute-start | bytes 147464 | tf_op jit(solution)/shard_map/ppermute | solution.py:19
  61.5 19.4 %collective-permute-start.5 = (bf16[3,32,256]{2,1,0:T(8,128)(2,1)}, bf16[3,32,256]{2,1,0:T(8,128)(2,1)S(1)}, u32[]{:S(2)}, u32[]{:S(2)}) collective-permute-start(bf16[3,32,256]{2,1,0:T(8,128)(2,1)} %get-tuple-element.33), channel_id=1, source_target_pairs={{8,0},{16,8},{24,16},{32,24},{40,32},{48,40},{56,48},{64,56},{72,6... | collective-permute-start | bytes 147464 | tf_op jit(solution)/shard_map/ppermute | solution.py:20
  65.7 125.0 %collective-permute-start.9 = (bf16[3,3,32,256]{3,2,1,0:T(8,128)(2,1)}, bf16[3,3,32,256]{3,2,1,0:T(8,128)(2,1)S(1)}, u32[]{:S(2)}, u32[]{:S(2)}) collective-permute-start(bf16[3,3,32,256]{3,2,1,0:T(8,128)(2,1)} %get-tuple-element.21), channel_id=1, source_target_pairs={{8,0},{16,8},{24,16},{32,24},{40,32},{48,40},{56,48},{64,56},{72,6... | collective-permute-start | bytes 442376 | tf_op jit(solution)/shard_map/ppermute | solution.py:20
  66.9 123.7 %collective-permute-start.8 = (bf16[3,3,32,256]{3,2,1,0:T(8,128)(2,1)}, bf16[3,3,32,256]{3,2,1,0:T(8,128)(2,1)}, u32[]{:S(2)}, u32[]{:S(2)}) collective-permute-start(bf16[3,3,32,256]{3,2,1,0:T(8,128)(2,1)} %get-tuple-element.20), channel_id=1, source_target_pairs={{0,8},{8,16},{16,24},{24,32},{32,40},{40,48},{48,56},{56,64},{64,7... | collective-permute-start | bytes 442376 | tf_op jit(solution)/shard_map/ppermute | solution.py:19
  180.9 41.5 %all-to-all-start.4 = ((bf16[16,2,32768]{2,1,0:T(2,128)(2,1)}), bf16[16,2,32768]{2,1,0:T(2,128)(2,1)}, u32[]{:S(2)}, u32[]{:S(2)}) async-start(bf16[16,2,32768]{2,1,0:T(2,128)(2,1)} %reshape.237), calls=%async_computation.4 | async-start | bytes 4194304 | tf_op jit(solution)/shard_map/all_to_all | solution.py:126
  186.7 10.0 %copy-start.3 = (bf16[8,32,32,32]{3,2,1,0:T(8,128)(2,1)S(1)}, bf16[8,32,32,32]{3,2,1,0:T(8,128)(2,1)}, u32[]{:S(2)}) copy-start(bf16[8,32,32,32]{3,2,1,0:T(8,128)(2,1)} %reshape_reshape.15) | copy-start | bytes 1572868
  186.7 19.2 %collective-permute-start = (bf16[3,32,256]{2,1,0:T(8,128)(2,1)S(1)}, bf16[3,32,256]{2,1,0:T(8,128)(2,1)S(1)}, u32[]{:S(2)}, u32[]{:S(2)}) collective-permute-start(bf16[3,32,256]{2,1,0:T(8,128)(2,1)S(1)} %slice.346), channel_id=1, source_target_pairs={{0,8},{8,16},{16,24},{24,32},{32,40},{40,48},{48,56},{56,64},{64,7... | collective-permute-start | bytes 147464 | tf_op jit(solution)/shard_map/ppermute | solution.py:19
  192.4 22.2 %collective-permute-start.11 = (bf16[3,38,3,256]{3,2,1,0:T(4,128)(2,1)}, bf16[3,38,3,256]{3,2,1,0:T(4,128)(2,1)}, u32[]{:S(2)}, u32[]{:S(2)}) collective-permute-start(bf16[3,38,3,256]{3,2,1,0:T(4,128)(2,1)} %get-tuple-element.19), channel_id=1, source_target_pairs={{1,0},{2,1},{3,2},{4,3},{5,4},{6,5},{7,6},{9,8},{10,9},{11,10},{12... | collective-permute-start | bytes 525320 | tf_op jit(solution)/shard_map/ppermute | solution.py:20
  194.3 20.3 %collective-permute-start.10 = (bf16[3,38,3,256]{3,2,1,0:T(4,128)(2,1)}, bf16[3,38,3,256]{3,2,1,0:T(4,128)(2,1)}, u32[]{:S(2)}, u32[]{:S(2)}) collective-permute-start(bf16[3,38,3,256]{3,2,1,0:T(4,128)(2,1)} %get-tuple-element.18), channel_id=1, source_target_pairs={{0,1},{1,2},{2,3},{3,4},{4,5},{5,6},{6,7},{8,9},{9,10},{10,11},{11... | collective-permute-start | bytes 525320 | tf_op jit(solution)/shard_map/ppermute | solution.py:19
  203.8 6.4 %collective-permute-start.1 = (bf16[3,32,256]{2,1,0:T(8,128)(2,1)S(1)}, bf16[3,32,256]{2,1,0:T(8,128)(2,1)S(1)}, u32[]{:S(2)}, u32[]{:S(2)}) collective-permute-start(bf16[3,32,256]{2,1,0:T(8,128)(2,1)S(1)} %slice.348), channel_id=1, source_target_pairs={{8,0},{16,8},{24,16},{32,24},{40,32},{48,40},{56,48},{64,56},{72,6... | collective-permute-start | bytes 147464 | tf_op jit(solution)/shard_map/ppermute | solution.py:20
  210.3 11.1 %collective-permute-start.3 = (bf16[38,3,256]{2,1,0:T(4,128)(2,1)S(1)}, bf16[38,3,256]{2,1,0:T(4,128)(2,1)S(1)}, u32[]{:S(2)}, u32[]{:S(2)}) collective-permute-start(bf16[38,3,256]{2,1,0:T(4,128)(2,1)S(1)} %get-tuple-element.30), channel_id=1, source_target_pairs={{1,0},{2,1},{3,2},{4,3},{5,4},{6,5},{7,6},{9,8},{10,9},{11,10},{12... | collective-permute-start | bytes 175112 | tf_op jit(solution)/shard_map/ppermute | solution.py:20
  212.3 9.1 %collective-permute-start.2 = (bf16[38,3,256]{2,1,0:T(4,128)(2,1)S(1)}, bf16[38,3,256]{2,1,0:T(4,128)(2,1)S(1)}, u32[]{:S(2)}, u32[]{:S(2)}) collective-permute-start(bf16[38,3,256]{2,1,0:T(4,128)(2,1)S(1)} %get-tuple-element.29), channel_id=1, source_target_pairs={{0,1},{1,2},{2,3},{3,4},{4,5},{5,6},{6,7},{8,9},{9,10},{10,11},{11... | collective-permute-start | bytes 175112 | tf_op jit(solution)/shard_map/ppermute | solution.py:19
  427.8 51.6 %all-to-all-start.6 = ((bf16[16,2,32768]{2,1,0:T(2,128)(2,1)}), bf16[16,2,32768]{2,1,0:T(2,128)(2,1)}, u32[]{:S(2)}, u32[]{:S(2)}) async-start(bf16[16,2,32768]{2,1,0:T(2,128)(2,1)} %convert_element_type.164), calls=%async_computation.6 | async-start | bytes 4194304 | tf_op jit(solution)/shard_map/all_to_all | solution.py:180
  444.8 25.0 %collective-permute-start.13 = (bf16[3,32,256]{2,1,0:T(8,128)(2,1)S(1)}, bf16[3,32,256]{2,1,0:T(8,128)(2,1)S(1)}, u32[]{:S(2)}, u32[]{:S(2)}) collective-permute-start(bf16[3,32,256]{2,1,0:T(8,128)(2,1)S(1)} %get-tuple-element.32), channel_id=1, source_target_pairs={{8,0},{16,8},{24,16},{32,24},{40,32},{48,40},{56,48},{64,56},{72,6... | collective-permute-start | bytes 147464 | tf_op jit(solution)/shard_map/ppermute | solution.py:20
  446.1 23.7 %collective-permute-start.12 = (bf16[3,32,256]{2,1,0:T(8,128)(2,1)S(1)}, bf16[3,32,256]{2,1,0:T(8,128)(2,1)S(1)}, u32[]{:S(2)}, u32[]{:S(2)}) collective-permute-start(bf16[3,32,256]{2,1,0:T(8,128)(2,1)S(1)} %get-tuple-element.31), channel_id=1, source_target_pairs={{0,8},{8,16},{16,24},{24,32},{32,40},{40,48},{48,56},{56,64},{64,7... | collective-permute-start | bytes 147464 | tf_op jit(solution)/shard_map/ppermute | solution.py:19
  451.8 22.7 %collective-permute-start.7 = (bf16[38,3,256]{2,1,0:T(4,128)(2,1)S(1)}, bf16[38,3,256]{2,1,0:T(4,128)(2,1)S(1)}, u32[]{:S(2)}, u32[]{:S(2)}) collective-permute-start(bf16[38,3,256]{2,1,0:T(4,128)(2,1)S(1)} %get-tuple-element.28), channel_id=1, source_target_pairs={{1,0},{2,1},{3,2},{4,3},{5,4},{6,5},{7,6},{9,8},{10,9},{11,10},{12... | collective-permute-start | bytes 175112 | tf_op jit(solution)/shard_map/ppermute | solution.py:20
  454.1 20.4 %collective-permute-start.6 = (bf16[38,3,256]{2,1,0:T(4,128)(2,1)S(1)}, bf16[38,3,256]{2,1,0:T(4,128)(2,1)S(1)}, u32[]{:S(2)}, u32[]{:S(2)}) collective-permute-start(bf16[38,3,256]{2,1,0:T(4,128)(2,1)S(1)} %get-tuple-element.27), channel_id=1, source_target_pairs={{0,1},{1,2},{2,3},{3,4},{4,5},{5,6},{6,7},{8,9},{9,10},{10,11},{11... | collective-permute-start | bytes 175112 | tf_op jit(solution)/shard_map/ppermute | solution.py:19
  470.0 8.0 %collective-permute-start.15 = (bf16[38,3,256]{2,1,0:T(4,128)(2,1)S(1)}, bf16[38,3,256]{2,1,0:T(4,128)(2,1)S(1)}, u32[]{:S(2)}, u32[]{:S(2)}) collective-permute-start(bf16[38,3,256]{2,1,0:T(4,128)(2,1)S(1)} %get-tuple-element.26), channel_id=1, source_target_pairs={{1,0},{2,1},{3,2},{4,3},{5,4},{6,5},{7,6},{9,8},{10,9},{11,10},{12... | collective-permute-start | bytes 175112 | tf_op jit(solution)/shard_map/ppermute | solution.py:20
  471.9 6.1 collective-permute-start.14
  567.3 49.8 %all-to-all-start.7 = ((bf16[16,2,32768]{2,1,0:T(2,128)(2,1)}), bf16[16,2,32768]{2,1,0:T(2,128)(2,1)}, u32[]{:S(2)}, u32[]{:S(2)}) async-start(bf16[16,2,32768]{2,1,0:T(2,128)(2,1)} %convert_element_type.176), calls=%async_computation.7 | async-start | bytes 4194304 | tf_op jit(solution)/shard_map/all_to_all | solution.py:180
  574.0 14.1 %copy-start.6 = (bf16[32,32,256]{2,1,0:T(8,128)(2,1)S(1)}, bf16[32,32,256]{2,1,0:T(8,128)(2,1)}, u32[]{:S(2)}) copy-start(bf16[32,32,256]{2,1,0:T(8,128)(2,1)} %get-tuple-element.7) | copy-start | bytes 1572868
  608.1 6.7 %copy-start.9 = (f32[1,32,32,256]{3,2,1,0:T(8,128)S(1)}, f32[1,32,32,256]{3,2,1,0:T(8,128)}, u32[]{:S(2)}) copy-start(f32[1,32,32,256]{3,2,1,0:T(8,128)} %get-tuple-element.23) | copy-start | bytes 3145732
  622.0 7.6 %copy-start.1 = (bf16[64,3,32,32]{0,3,2,1:T(8,128)(2,1)S(1)}, bf16[64,3,32,32]{0,3,2,1:T(8,128)(2,1)}, u32[]{:S(2)}) copy-start(bf16[64,3,32,32]{0,3,2,1:T(8,128)(2,1)} %param.10) | copy-start | bytes 1179652
  (10 other events, 50.9 us)
where the time goes:
time: 643 us; the launch traced here: 630 us
  local copies, waits for them, and re-layouts  305 us (47%)
  matrix products  142 us (22%)
  starting transfers between devices  83.6 us (13%)
  other arithmetic  57.8 us (9%)
  waiting for transfers between devices  39.6 us (6%)
    dot_general x4, matrix products, apply_operator(): jnp.einsum(forms_list[1], view_one, matrices[:, 1].astype(jnp.float32), p...  70.8 us
    reshape x4, local copies, waits for them, and re-layouts, apply_operator(): view_two = section_two.reshape(brick_total, edge_cells, square)  55 us
    reshape x4, local copies, waits for them, and re-layouts, apply_operator(): view_one = section_one.reshape(brick_total, edge_cells, square)  54.7 us
    convert_element_type x4, local copies, waits for them, and re-layouts, shards(): pulled = pulled.astype(jnp.bfloat16).reshape(peer_count, capacity, volume)  44.6 us
    convert_element_type x4, local copies, waits for them, and re-layouts, shards(): incoming = incoming.astype(jnp.bfloat16).reshape(slot_count, volume)  38.5 us
    dot_general x4, matrix products, apply_operator(): jnp.einsum(forms_list[0], bricks, matrices[:, 0], preferred_element_type=...  34.7 us
    ppermute x8, starting transfers between devices, extended(): before = lax.ppermute(last, axis, up)  27.2 us
    dot_general x4, matrix products, apply_operator(): jnp.einsum(forms_list[2], view_two, matrices[:, 2].astype(jnp.float32), p...  22.9 us
  transfers between devices with their start and end apart: 24, of which 8 were waited for; matrix products, arithmetic and copies ran while one was open for 31% of the time, Pallas kernels for 0%

commit v1 on v0

v1 whole, which is shorter than its diff:
```python
import jax
import jax.numpy as jnp
from jax import lax
from jax.experimental import pallas as pl
from jax.experimental.pallas import tpu as pltpu
from jax.sharding import PartitionSpec as P

MESH = pl.DeviceIdType.MESH
F32 = jnp.float32
BF16 = jnp.bfloat16
E = 32
CH = 256
HF = 128


def mm(a, b):
    return jnp.dot(a, b, preferred_element_type=F32)


def mmt(a, b):
    return lax.dot_general(a, b, (((1,), (1,)), ((), ())), preferred_element_type=F32)


def iota(shape, dim):
    return lax.broadcasted_iota(jnp.int32, shape, dim)


def kernel(
    idx_ref, tmpl, targ_hbm, vel_hbm, ops_ref, vg_hbm, tg_ref,
    f1, mv, gg, r3, r12, ps, pf, sel, lhs, wc, ost, mask, tile, dz, targ,
    qs0, qs1, qd, qv0, qv1, v2, out, s1f, l1f, hx, hxs, hy, meta, mz, my,
    xs, xr, hs, hr, ms, mr, ls,
):
    gx = lax.axis_index("gx")
    gy = lax.axis_index("gy")
    z = gx // 4
    y = gx % 4

    def at(dz_, dy_):
        return ((z + dz_) % 4) * 4 + (y + dy_) % 4

    xlo, xhi = (gx + 15) % 16, (gx + 1) % 16
    ylo, yhi = (gy + 7) % 8, (gy + 1) % 8
    peers = [at(1, 0), at(2, 0), at(3, 0), at(0, 1), at(0, 2), at(0, 3)]

    loads = [
        pltpu.make_async_copy(vel_hbm.at[0], qv0.at[pl.ds(3, E)], ls.at[0]),
        pltpu.make_async_copy(vel_hbm.at[1], qv1.at[:, pl.ds(8, E), :], ls.at[1]),
        pltpu.make_async_copy(vel_hbm.at[2], v2, ls.at[2]),
        pltpu.make_async_copy(targ_hbm, targ, ls.at[3]),
    ]
    for c in loads:
        c.start()

    barrier = pltpu.get_barrier_semaphore()
    for p in peers + [xlo, xhi]:
        pl.semaphore_signal(barrier, inc=1, device_id={"gx": p}, device_id_type=MESH)
    for p in (ylo, yhi):
        pl.semaphore_signal(barrier, inc=1, device_id={"gy": p}, device_id_type=MESH)

    lane_b = iota((8, 256), 1) // E
    row_t = iota((8, 256), 0)
    m = jnp.zeros((8, 256), jnp.int32)
    for t in range(2):
        for b in range(8):
            m = jnp.where((row_t == t) & (lane_b == b), idx_ref[1, t * 8 + b], m)
    meta[...] = m

    mask[...] = jnp.where(iota((256, 256), 0) // E == iota((256, 256), 1) // E, 1.0, 0.0).astype(BF16)
    tile[...] = jnp.where(iota((E, 256), 0) == iota((E, 256), 1) % E, 1.0, 0.0).astype(BF16)

    def build(t):
        for b in range(8):
            w = ops_ref[idx_ref[0, t * 8 + b]]
            for k in range(3):
                ost[t, k, b * E:(b + 1) * E, :] = w[k * E:(k + 1) * E, :]
        for k in range(2):
            for j in range(2):
                part = ost[t, k, j * 128:(j + 1) * 128, :]
                spread = mm(part, tile[:, 0:128]) * mask[0:128, 0:128].astype(F32)
                lhs[t, k, 0, j] = (spread[0:32] + spread[32:64] + spread[64:96] + spread[96:128]).astype(BF16)
                lhs[t, k, 1, j] = mmt(tile[:, 0:E], part).astype(BF16)
        wc[t] = (mm(ost[t, 2], tile[...]) * mask[...].astype(F32)).astype(BF16)

    build(0)

    pl.semaphore_wait(barrier, 10)

    sends = []

    def send(src, dst, ssem, rsem, dev):
        c = pltpu.make_async_remote_copy(
            src_ref=src, dst_ref=dst, send_sem=ssem, recv_sem=rsem, device_id=dev, device_id_type=MESH
        )
        return c

    metas = []
    for i, (buf, d) in enumerate([(mz, 1), (mz, 2), (mz, 3), (my, 1), (my, 2), (my, 3)]):
        dev = at(d, 0) if i < 3 else at(0, d)
        metas.append(send(meta, buf.at[3 - d], ms.at[i], mr.at[(0 if i < 3 else 3) + 3 - d], {"gx": dev}))
    for c in metas:
        c.start()

    def halo_x(f, low, high):
        return [
            send(low, hx.at[f, 1], hs.at[f, 0], hr.at[f, 0], {"gx": xlo}),
            send(high, hx.at[f, 0], hs.at[f, 1], hr.at[f, 1], {"gx": xhi}),
        ]

    def halo_y(f, low, high):
        return [
            send(low, hy.at[f, 1], hs.at[f, 2], hr.at[f, 2], {"gy": ylo}),
            send(high, hy.at[f, 0], hs.at[f, 3], hr.at[f, 3], {"gy": yhi}),
        ]

    def contract(t, k, tr, load, store):
        for i in range(8):
            for j in range(2):
                part = load(i, j)
                big = jnp.concatenate([part] * 4, axis=0) * mask[0:128, 0:128]
                store(i, j, mm(lhs[t, k, tr, j], big))

    def first(t, k, tr, row0, value):
        def load(i, j):
            return value[i * E:(i + 1) * E, j * 128:(j + 1) * 128]

        def store(i, j, res):
            f1[j, pl.ds(row0 + i * E, E), :] = res

        contract(t, k, tr, load, store)

    def second(t, k, tr, row0):
        got = [[None, None] for _ in range(8)]

        def load(i, j):
            return f1[j, pl.ds(row0 // E + i, E, stride=E), :].astype(BF16)

        def store(i, j, res):
            got[i][j] = res

        contract(t, k, tr, load, store)
        rows = [jnp.concatenate(g, axis=1) for g in got]
        return jnp.concatenate(rows, axis=0)

    def row_of(u):
        return pl.multiple_of((u % 2) * 512 + (u // 2) * CH, CH)

    def axes(p, u):
        a = (1 - u % 2) if p < 2 else u % 2
        gather = (at(a, 1 - a), at(3 * a, 3 * (1 - a)))
        scatter = (at(1 - a, a), at(3 * (1 - a), 3 * a))
        return gather, scatter

    def xcopy(p, u, n):
        (gp, gm), (sp, sm) = axes(p, u)
        own = mv.at[p, pl.ds(row_of(u), CH)]
        top, low = pl.ds(0, HF), pl.ds(HF, HF)
        src, dst, dev = [
            (own, gg.at[p, u, 0], gp),
            (own, gg.at[p, u, 1], gm),
            (gg.at[p, u, 0, top], gg.at[p, u, 2, top], gp),
            (gg.at[p, u, 1, low], gg.at[p, u, 2, low], gm),
            (ps.at[p, u, 0, top], r3.at[p, u, top], sp),
            (ps.at[p, u, 0, low], r3.at[p, u, low], sm),
            (ps.at[p, u, 1], r12.at[p, u, 0], sp),
            (ps.at[p, u, 2], r12.at[p, u, 1], sm),
        ][n]
        return send(src, dst, xs.at[p, u, n], xr.at[p, u, n], {"gx": dev})

    def units(body):
        def step(u, carry):
            body(u)
            return carry
        lax.fori_loop(0, 4, step, 0)

    def gather_start(p, u):
        xcopy(p, u, 0).start()
        xcopy(p, u, 1).start()

    def gather_on(p):
        def body(u):
            xcopy(p, u, 0).wait_recv()
            xcopy(p, u, 2).start()
            xcopy(p, u, 1).wait_recv()
            xcopy(p, u, 3).start()
        units(body)

    def pick(p, t):
        def body(u):
            xcopy(p, u, 2).wait_recv()
            xcopy(p, u, 3).wait_recv()
            h = u % 2
            blocks = [mv[p, pl.ds(row_of(u), CH), :], gg[p, u, 1], gg[p, u, 2], gg[p, u, 0]]

            def part(o):
                total = None
                for s in range(4):
                    v = mmt(blocks[s], sel[t, h, o, s]) if p < 2 else mm(blocks[s], sel[t, h, s, o])
                    total = v if total is None else total + v
                return total

            ps[p, u, 0] = part(2).astype(BF16)
            xcopy(p, u, 4).start()
            xcopy(p, u, 5).start()
            pf[u, 0] = part(1)
            pf[u, 1] = part(3)
            pf[u, 2] = part(0)
        units(body)

    def scatter_on(p):
        def body(u):
            xcopy(p, u, 4).wait_recv()
            ps[p, u, 1, 0:HF, :] = (pf[u, 0, 0:HF, :] + r3[p, u, 0:HF, :].astype(F32)).astype(BF16)
            ps[p, u, 1, HF:CH, :] = pf[u, 0, HF:CH, :].astype(BF16)
            xcopy(p, u, 6).start()
            xcopy(p, u, 5).wait_recv()
            ps[p, u, 2, 0:HF, :] = pf[u, 1, 0:HF, :].astype(BF16)
            ps[p, u, 2, HF:CH, :] = (pf[u, 1, HF:CH, :] + r3[p, u, HF:CH, :].astype(F32)).astype(BF16)
            xcopy(p, u, 7).start()
        units(body)

    def arrived(p, u):
        xcopy(p, u, 6).wait_recv()
        xcopy(p, u, 7).wait_recv()
        return pf[u, 2] + r12[p, u, 0].astype(F32) + r12[p, u, 1].astype(F32)

    def build_sel(t):
        row = iota((256, 256), 0)
        same = row % E == iota((256, 256), 1) % E
        row_e = row // E
        for h in range(2):
            for s in range(4):
                raw = (meta if s == 0 else (mz, my)[h].at[s - 1])[t:t + 1, :]
                rz, ry, e = raw >> 5, (raw >> 3) & 3, raw & 7
                if h == 0:
                    key = jnp.where(rz == z, (((ry - y) & 3) << 3) | e, -1)
                else:
                    key = jnp.where(ry == y, (((rz - z) & 3) << 3) | e, -1)
                key = jnp.broadcast_to(key, (256, 256))
                for o in range(4):
                    sel[t, h, o, s] = jnp.where(same & (row_e + 8 * o == key), 1.0, 0.0).astype(BF16)

    xl = jnp.where(gx > 0, 1.0, 0.0).astype(F32)
    xh = jnp.where(gx < 15, 1.0, 0.0).astype(F32)
    yl = jnp.where(gy > 0, 1.0, 0.0).astype(F32)
    yh = jnp.where(gy < 7, 1.0, 0.0).astype(F32)

    def rim_x(f, q, off):
        for i in range(3):
            q[i, off:off + E, :] = hx[f, 0, i * E:(i + 1) * E, :].astype(F32) * xl
            q[E + 3 + i, off:off + E, :] = hx[f, 1, i * E:(i + 1) * E, :].astype(F32) * xh

    def rim_y(f, q, off):
        def step(i, c):
            q[off + i, 0:8, :] = hy[f, 0, i] * yl
            q[off + i, 40:48, :] = hy[f, 1, i] * yh
            return c
        lax.fori_loop(0, E, step, 0)

    def combine(p1, m1, p2, m2, p3, m3):
        return 0.75 * (p1 - m1) - 0.15 * (p2 - m2) + (p3 - m3) * (1.0 / 60.0)

    def d_x(q, i, off):
        at_ = [q[i + n, off:off + E, :] for n in range(7)]
        return combine(at_[4], at_[2], at_[5], at_[1], at_[6], at_[0])

    def d_y(q, i):
        at_ = [q[i, 5 + n:5 + n + E, :] for n in range(7)]
        return combine(at_[4], at_[2], at_[5], at_[1], at_[6], at_[0])

    diff = iota((256, 256), 0) - iota((256, 256), 1)
    size = jnp.abs(diff)
    coef = jnp.where(size == 1, 0.75, 0.0) + jnp.where(size == 2, -0.15, 0.0) + jnp.where(size == 3, 1.0 / 60.0, 0.0)
    coef = jnp.where(diff < 0, -coef, coef).astype(F32)
    dz_hi = coef.astype(BF16)
    dz[0] = dz_hi
    dz[1] = (coef - dz_hi.astype(F32)).astype(BF16)

    def d_z(value, exact):
        hi = value.astype(BF16)
        total = mm(hi, dz[0]) + mm(hi, dz[1])
        if not exact:
            total = total + mm((value - hi.astype(F32)).astype(BF16), dz[0])
        return total

    def planes(lo, hi, body):
        def step(i, c):
            body(i)
            return c
        lax.fori_loop(lo, hi, step, 0)

    def gradient(q, weight, lo, hi, exact):
        def group(g):
            i0 = g * 8
            dzv = d_z(q[pl.ds(3 + i0, 8), 8:8 + E, :].reshape(8 * E, 256), exact)
            for n in range(8):
                i = i0 + n
                w = weight(i)
                part = dzv[n * E:(n + 1) * E]
                if w is None:
                    out[0, i] = -0.25 * d_x(q, i + 0, 8)
                    out[1, i] = -0.25 * d_y(q, i + 3)
                    out[2, i] = -0.25 * part
                else:
                    out[0, i] = out[0, i] + w * d_x(q, i, 8)
                    out[1, i] = out[1, i] + w * d_y(q, i + 3)
                    out[2, i] = out[2, i] + w * part
        planes(lo, hi, group)

    sends += halo_x(0, tmpl.at[pl.ds(0, 96)], tmpl.at[pl.ds(928, 96)])
    for c in sends:
        c.start()

    def chunk0(u):
        r = pl.multiple_of(u * CH, CH)
        first(0, 1, 0, r, tmpl[pl.ds(r, CH), :])
    units(chunk0)

    def forward_start(p, t, k):
        def body(u):
            r = row_of(u)
            mv[p, pl.ds(r, CH), :] = mmt(second(t, k, 0, r).astype(BF16), wc[t]).astype(BF16)
            gather_start(p, u)
        units(body)

    forward_start(0, 0, 0)

    def fill0(i):
        qs0[3 + i, 8:8 + E, :] = tmpl[pl.ds(pl.multiple_of(i * E, E), E), :].astype(F32)
    planes(0, E, fill0)
    for c in loads:
        c.wait()
    for i in range(3):
        hxs[0, 0, i * E:(i + 1) * E, :] = qv0[3 + i].astype(BF16)
        hxs[0, 1, i * E:(i + 1) * E, :] = qv0[E + i].astype(BF16)
    more = halo_y(0, qs0.at[pl.ds(3, E), pl.ds(8, 8), :], qs0.at[pl.ds(3, E), pl.ds(32, 8), :])
    more += halo_x(1, hxs.at[0, 0], hxs.at[0, 1])
    more += halo_y(1, qv1.at[:, pl.ds(8, 8), :], qv1.at[:, pl.ds(32, 8), :])
    for c in more:
        c.start()
    sends += more
    gather_on(0)
    for c in metas:
        c.wait_recv()
    build_sel(0)
    pick(0, 0)

    for c in more[2:6]:
        c.wait_recv()
    rim_x(1, qv0, 0)
    rim_y(1, qv1, 0)

    def div_group(g):
        i0 = g * 8
        dzv = d_z(v2[pl.ds(i0, 8)].reshape(8 * E, 256), False)
        for n in range(8):
            i = i0 + n
            qd[3 + i, 8:8 + E, :] = d_x(qv0, i, 0) + d_y(qv1, i) + dzv[n * E:(n + 1) * E]
    planes(0, 4, div_group)
    for i in range(3):
        hxs[1, 0, i * E:(i + 1) * E, :] = qd[3 + i, 8:8 + E, :].astype(BF16)
        hxs[1, 1, i * E:(i + 1) * E, :] = qd[E + i, 8:8 + E, :].astype(BF16)
    divs = halo_x(2, hxs.at[1, 0], hxs.at[1, 1])
    divs += halo_y(2, qd.at[pl.ds(3, E), pl.ds(8, 8), :], qd.at[pl.ds(3, E), pl.ds(32, 8), :])
    for c in divs:
        c.start()
    sends += divs
    scatter_on(0)
    build(1)

    def end0(u):
        r = row_of(u)
        s1 = arrived(0, u).astype(BF16)
        wide = s1.astype(F32)
        s1f[0, pl.ds(r, CH), :] = wide[:, 0:128]
        s1f[1, pl.ds(r, CH), :] = wide[:, 128:256]
        first(1, 0, 0, r, s1)
    units(end0)

    forward_start(1, 1, 1)

    def fill1(i):
        qs1[3 + i, 8:8 + E, 0:128] = s1f[0, pl.ds(i, E, stride=E), :]
        qs1[3 + i, 8:8 + E, 128:256] = s1f[1, pl.ds(i, E, stride=E), :]
    planes(0, E, fill1)
    for i in range(3):
        hxs[2, 0, i * E:(i + 1) * E, :] = qs1[3 + i, 8:8 + E, :].astype(BF16)
        hxs[2, 1, i * E:(i + 1) * E, :] = qs1[E + i, 8:8 + E, :].astype(BF16)
    ones = halo_x(3, hxs.at[2, 0], hxs.at[2, 1])
    ones += halo_y(3, qs1.at[pl.ds(3, E), pl.ds(8, 8), :], qs1.at[pl.ds(3, E), pl.ds(32, 8), :])
    for c in ones:
        c.start()
    sends += ones
    gather_on(1)
    build_sel(1)
    pick(1, 1)
    for c in divs:
        c.wait_recv()
    rim_x(2, qd, 8)
    rim_y(2, qd, 3)
    gradient(qd, lambda i: None, 0, 4, False)
    scatter_on(1)

    def end1(u):
        r = row_of(u)
        s2 = arrived(1, u).astype(BF16).astype(F32)
        mv[2, pl.ds(r, CH), :] = (s2 - targ[pl.ds(r, CH), :].astype(F32)).astype(BF16)
        gather_start(2, u)
    units(end1)

    for c in ones:
        c.wait_recv()
    rim_x(3, qs1, 8)
    rim_y(3, qs1, 3)

    def weight1(i):
        return 0.5 * mv[2, pl.ds(pl.multiple_of(i * E, E), E), :].astype(F32)
    gather_on(2)
    gradient(qs1, weight1, 0, 2, True)
    pick(2, 1)
    gradient(qs1, weight1, 2, 4, True)
    scatter_on(2)

    def end2(u):
        r = row_of(u)
        back = arrived(2, u).astype(BF16)
        first(1, 1, 1, r, mm(back, wc[1]).astype(BF16))
    units(end2)

    def adjoint_start(u):
        r = row_of(u)
        l1 = second(1, 0, 1, r).astype(BF16)
        mv[3, pl.ds(r, CH), :] = l1
        gather_start(3, u)
        wide = l1.astype(F32) * 0.5
        l1f[0, pl.ds(r, CH), :] = wide[:, 0:128]
        l1f[1, pl.ds(r, CH), :] = wide[:, 128:256]
    units(adjoint_start)

    for c in sends[0:4]:
        c.wait_recv()
    rim_x(0, qs0, 8)
    rim_y(0, qs0, 3)

    def weight0(i):
        return jnp.concatenate(
            [l1f[0, pl.ds(i, E, stride=E), :], l1f[1, pl.ds(i, E, stride=E), :]], axis=1
        )
    gather_on(3)
    gradient(qs0, weight0, 0, 2, True)
    pick(3, 0)
    gradient(qs0, weight0, 2, 4, True)
    save = pltpu.make_async_copy(out, vg_hbm, ls.at[4])
    save.start()
    scatter_on(3)

    def end3(u):
        r = row_of(u)
        back = arrived(3, u).astype(BF16)
        first(0, 0, 1, r, mm(back, wc[0]).astype(BF16))
    units(end3)

    def finish(u):
        r = row_of(u)
        tg_ref[pl.ds(r, CH), :] = second(0, 1, 1, r).astype(BF16)
    units(finish)

    for c in metas + sends:
        c.wait_send()
    for p in range(4):
        def drain(u, p=p):
            for n in range(8):
                xcopy(p, u, n).wait_send()
        units(drain)
    save.wait()


def shards(template, target_image, velocity, operators, route, target_brick, operator_index):
    index = jnp.stack(
        [operator_index.reshape(16), route.reshape(16) * 8 + target_brick.reshape(16)]
    )
    vmem = pl.BlockSpec(memory_space=pltpu.VMEM)
    hbm = pl.BlockSpec(memory_space=pl.ANY)
    field = (E + 6, E + 16, 256)
    dma = pltpu.SemaphoreType.DMA
    vg, tg = pl.pallas_call(
        kernel,
        out_shape=(
            jax.ShapeDtypeStruct((3, E, E, 256), F32),
            jax.ShapeDtypeStruct((1024, 256), BF16),
        ),
        in_specs=[pl.BlockSpec(memory_space=pltpu.SMEM), vmem, hbm, hbm, vmem],
        out_specs=(hbm, vmem),
        scratch_shapes=[
            pltpu.VMEM((2, 1024, 128), F32),
            pltpu.VMEM((4, 1024, 256), BF16),
            pltpu.VMEM((4, 4, 3, CH, 256), BF16),
            pltpu.VMEM((4, 4, CH, 256), BF16),
            pltpu.VMEM((4, 4, 2, CH, 256), BF16),
            pltpu.VMEM((4, 4, 3, CH, 256), BF16),
            pltpu.VMEM((4, 3, CH, 256), F32),
            pltpu.VMEM((2, 2, 4, 4, 256, 256), BF16),
            pltpu.VMEM((2, 2, 2, 2, E, 128), BF16),
            pltpu.VMEM((2, 256, 256), BF16),
            pltpu.VMEM((2, 3, 256, E), BF16),
            pltpu.VMEM((256, 256), BF16),
            pltpu.VMEM((E, 256), BF16),
            pltpu.VMEM((2, 256, 256), BF16),
            pltpu.VMEM((1024, 256), BF16),
            pltpu.VMEM(field, F32),
            pltpu.VMEM(field, F32),
            pltpu.VMEM(field, F32),
            pltpu.VMEM((E + 6, E, 256), F32),
            pltpu.VMEM((E, E + 16, 256), F32),
            pltpu.VMEM((E, E, 256), F32),
            pltpu.VMEM((3, E, E, 256), F32),
            pltpu.VMEM((2, 1024, 128), F32),
            pltpu.VMEM((2, 1024, 128), F32),
            pltpu.VMEM((4, 2, 96, 256), BF16),
            pltpu.VMEM((3, 2, 96, 256), BF16),
            pltpu.VMEM((4, 2, E, 8, 256), F32),
            pltpu.VMEM((8, 256), jnp.int32),
            pltpu.VMEM((3, 8, 256), jnp.int32),
            pltpu.VMEM((3, 8, 256), jnp.int32),
            dma((4, 4, 8)),
            dma((4, 4, 8)),
            dma((4, 4)),
            dma((4, 4)),
            dma((6,)),
            dma((6,)),
            dma((5,)),
        ],
        compiler_params=pltpu.CompilerParams(
            collective_id=0, has_side_effects=True, vmem_limit_bytes=62 << 20
        ),
        name="gradient",
    )(
        index,
        template.reshape(1024, 256),
        target_image.reshape(1024, 256),
        velocity,
        operators.reshape(64, 96, E),
    )
    return vg, tg.reshape(E, E, 256)


def solution(mesh):
    placed = (
        P("gx", "gy", None),
        P("gx", "gy", None),
        P(None, "gx", "gy", None),
        P(),
        P(None, "gx", "gy", None, None),
        P(None, "gx", "gy", None),
        P(None, "gx", "gy", None),
    )
    return jax.shard_map(
        shards,
        mesh=mesh,
        in_specs=placed,
        out_specs=(P(None, "gx", "gy", None), P("gx", "gy", None)),
        check_vma=False,
    )
```

time: 643 us -> 124 us (0.19); the launches traced: 630 us -> 123 us
  local copies, waits for them, and re-layouts: 305 us -> 8.61 us
  matrix products: 142 us -> 0 us
  Pallas kernels: 0 us -> 110 us
  starting transfers between devices: 83.6 us -> 0 us
  other arithmetic: 57.8 us -> 3.96 us
  waiting for transfers between devices: 39.6 us -> 0 us
    reshape x22 -> x1, local copies, waits for them, and re-layouts: 154 us -> 0.08 us  [shards(): target_brick.reshape(16)]
    dot_general x22 -> x0, matrix products: 142 us -> none  [the longest x4 70.8 us: apply_operator(): jnp.einsum(forms_list[1], view_one, matrices[:, 1].astype(jnp.float32), p...]
    convert_element_type x14 -> x0, local copies, waits for them, and re-layouts: 116 us -> none  [the longest x4 44.6 us: shards(): pulled = pulled.astype(jnp.bfloat16).reshape(peer_count, capacity, volume)]
    pallas_call x0 -> x1, Pallas kernels: none -> 110 us  [shards(): pl.pallas_call(kernel, out_shape=(jax.ShapeDtypeStruct((3, E, E, 256), F3...]
    all_to_all x8 -> x0, starting transfers between devices: 43 us -> none  [the longest x2 15.1 us: shards(): lax.all_to_all(pulled, 'gx', split_axis=0, concat_axis=0, tiled=True)]
    ppermute x16 -> x0, starting transfers between devices: 40.6 us -> none  [the longest x8 27.2 us: extended(): before = lax.ppermute(last, axis, up)]
    another operation x4 -> x1, other arithmetic: 29.3 us -> 0.57 us  [shards(): jnp.stack([operator_index.reshape(16), route.reshape(16) * 8 + target_bri...]
    all_to_all x8 -> x0, waiting for transfers between devices: 20.8 us -> none  [the longest x2 8.94 us: shards(): lax.all_to_all(slot_landing, 'gx', split_axis=0, concat_axis=0, tiled=True)]
  transfers between devices with their start and end apart: 24 -> 0, of which waited for: 8 -> 0; matrix products, arithmetic and copies ran while one was open for 31% -> 0% of each run, Pallas kernels for 0% -> 0%
where the time goes in v1:
time: 124 us; the launch traced here: 123 us
  Pallas kernels  110 us (89%)
  local copies, waits for them, and re-layouts  8.61 us (7%)
  other arithmetic  3.96 us (3%)
    pallas_call x1, Pallas kernels, shards(): pl.pallas_call(kernel, out_shape=(jax.ShapeDtypeStruct((3, E, E, 256), F3...  110 us
    unnamed x6, local copies, waits for them, and re-layouts  8.36 us
    unnamed x2, other arithmetic  2.68 us

profile of v1, /device:TPU:2, one launch (start us, length us, event | category | flops | bytes accessed | tf_op | source)
XLA Modules:
  0.0 123.4 jit_solution(16912595887346724561)
XLA Ops:
  0.6 0.7 multiply_reduce_fusion
  1.3 0.1 mul.14
  1.4 0.5 broadcast.23
  1.9 1.3 %reduce.10 = s32[2,8]{1,0:T(2,128)S(1)} reduce(s32[2,1,1,8]{3,2,1,0:T(1,128)} %param.12, s32[]{:T(128)} %broadcast.23), dimensions={1,2}, to_apply=%param.12.reduce_sub_computation.3 | reduce | bytes 132 | tf_op args[5]
  3.3 0.1 reshape.42
  3.4 1.3 %reduce.11 = s32[2,8]{1,0:T(2,128)S(1)} reduce(s32[2,1,1,8]{3,2,1,0:T(1,128)} %param.13, s32[]{:T(128)} %broadcast.23), dimensions={1,2}, to_apply=%param.13.reduce_sub_computation.3 | reduce | bytes 132 | tf_op args[6]
  4.7 0.1 stack_reshape.3
  4.8 0.6 pad_add_fusion.idx_ref
  5.4 3.0 %copy.9 = bf16[64,3,32,32]{3,2,1,0:T(8,128)(2,1)} copy(bf16[64,3,32,32]{0,3,2,1:T(8,128)(2,1)} %param.10) | data formatting | bytes 786432 | tf_op args[3]
  8.4 110.2 %gradient.1 = (f32[3,32,32,256]{3,2,1,0:T(8,128)}, bf16[1024,256]{1,0:T(8,128)(2,1)}) custom-call(s32[2,16]{1,0:T(2,128)} %pad_add_fusion.idx_ref, bf16[1024,256]{1,0:T(8,128)(2,1)} %bitcast.5, bf16[1024,256]{1,0:T(8,128)(2,1)} %bitcast.6, f32[3,32,32,256]{3,2,1,0:T(8,128)} %vel_hbm.1, bf16[64,96,32]{2,1,0:T(8,128)(2,1)} %bitcast.4), custom_call_target="tpu_custom_call" | custom-call | tf_op jit(solution)/shard_map/gradient/pallas_call | solution.py:486
  118.6 0.0 copy-start
  118.6 4.0 %copy.12 = f32[3,32,32,256]{3,2,1,0:T(8,128)} copy(f32[3,32,32,256]{3,2,1,0:T(8,128)} %get-tuple-element.8) | data formatting | bytes 6291456
  122.6 0.0 copy-done
  122.6 0.8 copy.13
  (1 shorter events, 0.0 us)
Async XLA Ops:
  118.6 4.0 %copy-start = (bf16[1024,256]{1,0:T(8,128)(2,1)S(1)}, bf16[1024,256]{1,0:T(8,128)(2,1)}, u32[]{:S(2)}) copy-start(bf16[1024,256]{1,0:T(8,128)(2,1)} %get-tuple-element.5) | copy-start | bytes 1572868

commit v2 on v1

--- a/solution.py
+++ b/solution.py
@@ -26,10 +26,11 @@
 
 
 def kernel(
-    idx_ref, tmpl, targ_hbm, vel_hbm, ops_ref, vg_hbm, tg_ref,
-    f1, mv, gg, r3, r12, ps, pf, sel, lhs, wc, ost, mask, tile, dz, targ,
+    opi_ref, route_ref, brick_ref, tmpl_hbm, targ_hbm, vel_hbm, ops_hbm, vg_hbm, tg_ref,
+    tmpl, ops_ref,
+    f1, gg, r3, r12, ps, pf, sel, lhs, wc, ost, chosen, fold, mask, mask4, tile, dz, targ,
     qs0, qs1, qd, qv0, qv1, v2, out, s1f, l1f, hx, hxs, hy, meta, mz, my,
-    xs, xr, hs, hr, ms, mr, ls,
+    xs, xr, hs, hs2, hr, ms, mr, ls,
 ):
     gx = lax.axis_index("gx")
     gy = lax.axis_index("gy")
@@ -39,41 +40,61 @@
     def at(dz_, dy_):
         return ((z + dz_) % 4) * 4 + (y + dy_) % 4
 
-    xlo, xhi = (gx + 15) % 16, (gx + 1) % 16
     ylo, yhi = (gy + 7) % 8, (gy + 1) % 8
-    peers = [at(1, 0), at(2, 0), at(3, 0), at(0, 1), at(0, 2), at(0, 3)]
-
+    peers = [at(1, 0), at(3, 0), at(0, 1), at(0, 3)]
+
+    barrier = pltpu.get_barrier_semaphore()
+    for p in peers:
+        pl.semaphore_signal(barrier, inc=1, device_id={"gx": p}, device_id_type=MESH)
+    for p in (ylo, yhi):
+        pl.semaphore_signal(barrier, inc=1, device_id={"gy": p}, device_id_type=MESH)
+
+    tables = [
+        pltpu.make_async_copy(ops_hbm, ops_ref, ls.at[5]),
+        pltpu.make_async_copy(tmpl_hbm, tmpl, ls.at[6]),
+    ]
     loads = [
         pltpu.make_async_copy(vel_hbm.at[0], qv0.at[pl.ds(3, E)], ls.at[0]),
         pltpu.make_async_copy(vel_hbm.at[1], qv1.at[:, pl.ds(8, E), :], ls.at[1]),
         pltpu.make_async_copy(vel_hbm.at[2], v2, ls.at[2]),
         pltpu.make_async_copy(targ_hbm, targ, ls.at[3]),
     ]
-    for c in loads:
+    for c in tables + loads:
         c.start()
-
-    barrier = pltpu.get_barrier_semaphore()
-    for p in peers + [xlo, xhi]:
-        pl.semaphore_signal(barrier, inc=1, device_id={"gx": p}, device_id_type=MESH)
-    for p in (ylo, yhi):
-        pl.semaphore_signal(barrier, inc=1, device_id={"gy": p}, device_id_type=MESH)
 
     lane_b = iota((8, 256), 1) // E
     row_t = iota((8, 256), 0)
     m = jnp.zeros((8, 256), jnp.int32)
     for t in range(2):
         for b in range(8):
-            m = jnp.where((row_t == t) & (lane_b == b), idx_ref[1, t * 8 + b], m)
+            m = jnp.where((row_t == t) & (lane_b == b), route_ref[t, 0, 0, b] * 8 + brick_ref[t, 0, 0, b], m)
     meta[...] = m
 
     mask[...] = jnp.where(iota((256, 256), 0) // E == iota((256, 256), 1) // E, 1.0, 0.0).astype(BF16)
+    mask4[...] = jnp.concatenate([mask[0:128, 0:128]] * 2, axis=1)
     tile[...] = jnp.where(iota((E, 256), 0) == iota((E, 256), 1) % E, 1.0, 0.0).astype(BF16)
 
+    fold[...] = jnp.where(iota((1024, E), 0) % E == iota((1024, E), 1), 1.0, 0.0).astype(BF16)
+    entry = iota((16, 64), 1)
+    row16 = iota((16, 64), 0)
+    hot = jnp.zeros((16, 64), F32)
+    for t in range(2):
+        for b in range(8):
+            hot = jnp.where((row16 == t * 8 + b) & (entry == opi_ref[t, 0, 0, b]), 1.0, hot)
+    hot = hot.astype(BF16)
+    tables[0].wait()
+    for k in range(3):
+        for n in range(4):
+            chosen[k, :, n * 256:(n + 1) * 256] = mmt(hot, ops_ref[k * 1024 + n * 256:k * 1024 + (n + 1) * 256, :])
+
     def build(t):
-        for b in range(8):
-            w = ops_ref[idx_ref[0, t * 8 + b]]
-            for k in range(3):
-                ost[t, k, b * E:(b + 1) * E, :] = w[k * E:(k + 1) * E, :]
+        for k in range(3):
+            keep = iota((E, 1024), 1) // E == iota((E, 1024), 0)
+            rows = [
+                jnp.where(keep, jnp.broadcast_to(chosen[k, t * 8 + b:t * 8 + b + 1, :], (E, 1024)), 0.0).astype(BF16)
+                for b in range(8)
+            ]
+            ost[t, k] = mm(jnp.concatenate(rows, axis=0), fold[...]).astype(BF16)
         for k in range(2):
             for j in range(2):
                 part = ost[t, k, j * 128:(j + 1) * 128, :]
@@ -84,8 +105,6 @@
 
     build(0)
 
-    pl.semaphore_wait(barrier, 10)
-
     sends = []
 
     def send(src, dst, ssem, rsem, dev):
@@ -94,31 +113,58 @@
         )
         return c
 
-    metas = []
-    for i, (buf, d) in enumerate([(mz, 1), (mz, 2), (mz, 3), (my, 1), (my, 2), (my, 3)]):
+    def meta_copy(i):
+        buf, half = ((mz, 0), (my, 3))[i // 3]
+        n = i % 3
+        d = (1, 3, 3)[n]
+        src, dst = [(meta, buf.at[2]), (meta, buf.at[0]), (buf.at[0], buf.at[1])][n]
         dev = at(d, 0) if i < 3 else at(0, d)
-        metas.append(send(meta, buf.at[3 - d], ms.at[i], mr.at[(0 if i < 3 else 3) + 3 - d], {"gx": dev}))
-    for c in metas:
-        c.start()
+        return send(src, dst, ms.at[i], mr.at[i], {"gx": dev})
+
+    metas = [meta_copy(i) for i in range(6)]
 
     def halo_x(f, low, high):
+        to_low, to_high = jnp.where(y == 0, 1, 0), jnp.where(y == 3, 1, 0)
         return [
-            send(low, hx.at[f, 1], hs.at[f, 0], hr.at[f, 0], {"gx": xlo}),
-            send(high, hx.at[f, 0], hs.at[f, 1], hr.at[f, 1], {"gx": xhi}),
+            send(low, hx.at[f, 1, to_low], hs.at[f, 0], hr.at[f, 0, to_low], {"gx": at(0, 3)}),
+            send(high, hx.at[f, 0, to_high], hs.at[f, 1], hr.at[f, 1, to_high], {"gx": at(0, 1)}),
         ]
+
+    def relay(f, n):
+        side = 1 - n
+        return send(
+            hx.at[f, side, 1], hx.at[f, side, 0], hs2.at[f, n], hr.at[f, n, 0], {"gx": at((3, 1)[n], 0)}
+        )
+
+    def hand_on(f):
+        @pl.when(y == 3)
+        def _():
+            send(hx.at[f, 1, 1], hx.at[f, 1, 1], hs2.at[f, 0], hr.at[f, 0, 1], {"gx": at(0, 1)}).wait_recv()
+            relay(f, 0).start()
+
+        @pl.when(y == 0)
+        def _():
+            send(hx.at[f, 0, 1], hx.at[f, 0, 1], hs2.at[f, 1], hr.at[f, 1, 1], {"gx": at(0, 3)}).wait_recv()
+            relay(f, 1).start()
+
+    def wait_x(f):
+        relay(f, 0).wait_recv()
+        relay(f, 1).wait_recv()
 
     def halo_y(f, low, high):
         return [
-            send(low, hy.at[f, 1], hs.at[f, 2], hr.at[f, 2], {"gy": ylo}),
-            send(high, hy.at[f, 0], hs.at[f, 3], hr.at[f, 3], {"gy": yhi}),
+            send(low, hy.at[f, 1], hs.at[f, 2], hr.at[f, 2, 0], {"gy": ylo}),
+            send(high, hy.at[f, 0], hs.at[f, 3], hr.at[f, 3, 0], {"gy": yhi}),
         ]
 
     def contract(t, k, tr, load, store):
-        for i in range(8):
-            for j in range(2):
-                part = load(i, j)
-                big = jnp.concatenate([part] * 4, axis=0) * mask[0:128, 0:128]
-                store(i, j, mm(lhs[t, k, tr, j], big))
+        for j in range(2):
+            for i in range(0, 8, 2):
+                part = jnp.concatenate([load(i, j), load(i + 1, j)], axis=1)
+                big = jnp.concatenate([part] * 4, axis=0) * mask4[...]
+                res = mm(lhs[t, k, tr, j], big)
+                store(i, j, res[:, 0:128])
+                store(i + 1, j, res[:, 128:256])
 
     def first(t, k, tr, row0, value):
         def load(i, j):
@@ -153,17 +199,19 @@
 
     def xcopy(p, u, n):
         (gp, gm), (sp, sm) = axes(p, u)
-        own = mv.at[p, pl.ds(row_of(u), CH)]
+        own, up, far, down = [gg.at[p, u, :, pl.ds(n * 256, 256)] for n in range(4)]
         top, low = pl.ds(0, HF), pl.ds(HF, HF)
         src, dst, dev = [
-            (own, gg.at[p, u, 0], gp),
-            (own, gg.at[p, u, 1], gm),
-            (gg.at[p, u, 0, top], gg.at[p, u, 2, top], gp),
-            (gg.at[p, u, 1, low], gg.at[p, u, 2, low], gm),
+            (own, down, gp),
+            (own, up, gm),
+            (down.at[top], far.at[top], gp),
+            (up.at[low], far.at[low], gm),
             (ps.at[p, u, 0, top], r3.at[p, u, top], sp),
             (ps.at[p, u, 0, low], r3.at[p, u, low], sm),
-            (ps.at[p, u, 1], r12.at[p, u, 0], sp),
-            (ps.at[p, u, 2], r12.at[p, u, 1], sm),
+            (ps.at[p, u, 1, top], r12.at[p, u, 0, top], sp),
+            (ps.at[p, u, 2, low], r12.at[p, u, 1, low], sm),
+            (ps.at[p, u, 1, low], r12.at[p, u, 0, low], sp),
+            (ps.at[p, u, 2, top], r12.at[p, u, 1, top], sm),
         ][n]
         return send(src, dst, xs.at[p, u, n], xr.at[p, u, n], {"gx": dev})
 
@@ -190,39 +238,43 @@
             xcopy(p, u, 2).wait_recv()
             xcopy(p, u, 3).wait_recv()
             h = u % 2
-            blocks = [mv[p, pl.ds(row_of(u), CH), :], gg[p, u, 1], gg[p, u, 2], gg[p, u, 0]]
+            held = [gg[p, u, :, n * 256:(n + 1) * 256] for n in range(4)]
 
             def part(o):
                 total = None
                 for s in range(4):
-                    v = mmt(blocks[s], sel[t, h, o, s]) if p < 2 else mm(blocks[s], sel[t, h, s, o])
+                    v = mmt(held[s], sel[t, h, o, s]) if p < 2 else mm(held[s], sel[t, h, s, o])
                     total = v if total is None else total + v
                 return total
 
             ps[p, u, 0] = part(2).astype(BF16)
             xcopy(p, u, 4).start()
             xcopy(p, u, 5).start()
-            pf[u, 0] = part(1)
-            pf[u, 1] = part(3)
-            pf[u, 2] = part(0)
+            v = part(1)
+            pf[u, 0, 0:HF, :] = v[0:HF]
+            ps[p, u, 1, HF:CH, :] = v[HF:CH].astype(BF16)
+            v = part(3)
+            pf[u, 0, HF:CH, :] = v[HF:CH]
+            ps[p, u, 2, 0:HF, :] = v[0:HF].astype(BF16)
+            pf[u, 1] = part(0)
         units(body)
 
     def scatter_on(p):
         def body(u):
+            xcopy(p, u, 8).start()
+            xcopy(p, u, 9).start()
             xcopy(p, u, 4).wait_recv()
             ps[p, u, 1, 0:HF, :] = (pf[u, 0, 0:HF, :] + r3[p, u, 0:HF, :].astype(F32)).astype(BF16)
-            ps[p, u, 1, HF:CH, :] = pf[u, 0, HF:CH, :].astype(BF16)
             xcopy(p, u, 6).start()
             xcopy(p, u, 5).wait_recv()
-            ps[p, u, 2, 0:HF, :] = pf[u, 1, 0:HF, :].astype(BF16)
-            ps[p, u, 2, HF:CH, :] = (pf[u, 1, HF:CH, :] + r3[p, u, HF:CH, :].astype(F32)).astype(BF16)
+            ps[p, u, 2, HF:CH, :] = (pf[u, 0, HF:CH, :] + r3[p, u, HF:CH, :].astype(F32)).astype(BF16)
             xcopy(p, u, 7).start()
         units(body)
 
     def arrived(p, u):
-        xcopy(p, u, 6).wait_recv()
-        xcopy(p, u, 7).wait_recv()
-        return pf[u, 2] + r12[p, u, 0].astype(F32) + r12[p, u, 1].astype(F32)
+        for n in (8, 9, 6, 7):
+            xcopy(p, u, n).wait_recv()
+        return pf[u, 1] + r12[p, u, 0].astype(F32) + r12[p, u, 1].astype(F32)
 
     def build_sel(t):
         row = iota((256, 256), 0)
@@ -247,8 +299,8 @@
 
     def rim_x(f, q, off):
         for i in range(3):
-            q[i, off:off + E, :] = hx[f, 0, i * E:(i + 1) * E, :].astype(F32) * xl
-            q[E + 3 + i, off:off + E, :] = hx[f, 1, i * E:(i + 1) * E, :].astype(F32) * xh
+            q[i, off:off + E, :] = hx[f, 0, 0, i * E:(i + 1) * E, :].astype(F32) * xl
+            q[E + 3 + i, off:off + E, :] = hx[f, 1, 0, i * E:(i + 1) * E, :].astype(F32) * xh
 
     def rim_y(f, q, off):
         def step(i, c):
@@ -307,46 +359,59 @@
                     out[2, i] = out[2, i] + w * part
         planes(lo, hi, group)
 
-    sends += halo_x(0, tmpl.at[pl.ds(0, 96)], tmpl.at[pl.ds(928, 96)])
-    for c in sends:
-        c.start()
+    tables[1].wait()
 
     def chunk0(u):
         r = pl.multiple_of(u * CH, CH)
         first(0, 1, 0, r, tmpl[pl.ds(r, CH), :])
     units(chunk0)
 
+    def fill0(i):
+        qs0[3 + i, 8:8 + E, :] = tmpl[pl.ds(pl.multiple_of(i * E, E), E), :].astype(F32)
+    planes(0, E, fill0)
+
+    pl.semaphore_wait(barrier, 6)
+
+    for i in (0, 1, 3, 4):
+        metas[i].start()
+
     def forward_start(p, t, k):
         def body(u):
             r = row_of(u)
-            mv[p, pl.ds(r, CH), :] = mmt(second(t, k, 0, r).astype(BF16), wc[t]).astype(BF16)
+            gg[p, u, :, 0:256] = mmt(second(t, k, 0, r).astype(BF16), wc[t]).astype(BF16)
             gather_start(p, u)
         units(body)
 
     forward_start(0, 0, 0)
 
-    def fill0(i):
-        qs0[3 + i, 8:8 + E, :] = tmpl[pl.ds(pl.multiple_of(i * E, E), E), :].astype(F32)
-    planes(0, E, fill0)
     for c in loads:
         c.wait()
     for i in range(3):
         hxs[0, 0, i * E:(i + 1) * E, :] = qv0[3 + i].astype(BF16)
         hxs[0, 1, i * E:(i + 1) * E, :] = qv0[E + i].astype(BF16)
-    more = halo_y(0, qs0.at[pl.ds(3, E), pl.ds(8, 8), :], qs0.at[pl.ds(3, E), pl.ds(32, 8), :])
-    more += halo_x(1, hxs.at[0, 0], hxs.at[0, 1])
-    more += halo_y(1, qv1.at[:, pl.ds(8, 8), :], qv1.at[:, pl.ds(32, 8), :])
-    for c in more:
+    velx = halo_x(1, hxs.at[0, 0], hxs.at[0, 1])
+    vels = halo_y(1, qv1.at[:, pl.ds(8, 8), :], qv1.at[:, pl.ds(32, 8), :])
+    tempx = halo_x(0, tmpl.at[pl.ds(0, 96)], tmpl.at[pl.ds(928, 96)])
+    temps = halo_y(0, qs0.at[pl.ds(3, E), pl.ds(8, 8), :], qs0.at[pl.ds(3, E), pl.ds(32, 8), :])
+    for c in velx + vels + tempx + temps:
         c.start()
-    sends += more
+    sends += velx + vels + tempx + temps
+    for i in (1, 4):
+        metas[i].wait_recv()
+        metas[i + 1].start()
+    for i in (0, 3, 2, 5):
+        metas[i].wait_recv()
+    build_sel(0)
     gather_on(0)
-    for c in metas:
+    hand_on(1)
+    hand_on(0)
+    build(1)
+    pick(0, 0)
+    scatter_on(0)
+
+    for c in vels:
         c.wait_recv()
-    build_sel(0)
-    pick(0, 0)
-
-    for c in more[2:6]:
-        c.wait_recv()
+    wait_x(1)
     rim_x(1, qv0, 0)
     rim_y(1, qv1, 0)
 
@@ -360,13 +425,12 @@
     for i in range(3):
         hxs[1, 0, i * E:(i + 1) * E, :] = qd[3 + i, 8:8 + E, :].astype(BF16)
         hxs[1, 1, i * E:(i + 1) * E, :] = qd[E + i, 8:8 + E, :].astype(BF16)
-    divs = halo_x(2, hxs.at[1, 0], hxs.at[1, 1])
-    divs += halo_y(2, qd.at[pl.ds(3, E), pl.ds(8, 8), :], qd.at[pl.ds(3, E), pl.ds(32, 8), :])
-    for c in divs:
+    divx = halo_x(2, hxs.at[1, 0], hxs.at[1, 1])
+    divs = halo_y(2, qd.at[pl.ds(3, E), pl.ds(8, 8), :], qd.at[pl.ds(3, E), pl.ds(32, 8), :])
+    for c in divx + divs:
         c.start()
-    sends += divs
-    scatter_on(0)
-    build(1)
+    sends += divx + divs
+    build_sel(1)
 
     def end0(u):
         r = row_of(u)
@@ -386,40 +450,44 @@
     for i in range(3):
         hxs[2, 0, i * E:(i + 1) * E, :] = qs1[3 + i, 8:8 + E, :].astype(BF16)
         hxs[2, 1, i * E:(i + 1) * E, :] = qs1[E + i, 8:8 + E, :].astype(BF16)
-    ones = halo_x(3, hxs.at[2, 0], hxs.at[2, 1])
-    ones += halo_y(3, qs1.at[pl.ds(3, E), pl.ds(8, 8), :], qs1.at[pl.ds(3, E), pl.ds(32, 8), :])
-    for c in ones:
+    onex = halo_x(3, hxs.at[2, 0], hxs.at[2, 1])
+    ones = halo_y(3, qs1.at[pl.ds(3, E), pl.ds(8, 8), :], qs1.at[pl.ds(3, E), pl.ds(32, 8), :])
+    for c in onex + ones:
         c.start()
-    sends += ones
+    sends += onex + ones
     gather_on(1)
-    build_sel(1)
+    hand_on(2)
     pick(1, 1)
+    hand_on(3)
+    scatter_on(1)
     for c in divs:
         c.wait_recv()
+    wait_x(2)
     rim_x(2, qd, 8)
     rim_y(2, qd, 3)
     gradient(qd, lambda i: None, 0, 4, False)
-    scatter_on(1)
 
     def end1(u):
         r = row_of(u)
         s2 = arrived(1, u).astype(BF16).astype(F32)
-        mv[2, pl.ds(r, CH), :] = (s2 - targ[pl.ds(r, CH), :].astype(F32)).astype(BF16)
+        gg[2, u, :, 0:256] = (s2 - targ[pl.ds(r, CH), :].astype(F32)).astype(BF16)
         gather_start(2, u)
     units(end1)
 
     for c in ones:
         c.wait_recv()
+    wait_x(3)
     rim_x(3, qs1, 8)
     rim_y(3, qs1, 3)
 
     def weight1(i):
-        return 0.5 * mv[2, pl.ds(pl.multiple_of(i * E, E), E), :].astype(F32)
+        u = (i % 16) // 8 * 2 + i // 16
+        return 0.5 * gg[2, u, pl.ds(pl.multiple_of(i % 8 * E, E), E), 0:256].astype(F32)
+    gradient(qs1, weight1, 0, 2, True)
     gather_on(2)
-    gradient(qs1, weight1, 0, 2, True)
     pick(2, 1)
+    scatter_on(2)
     gradient(qs1, weight1, 2, 4, True)
-    scatter_on(2)
 
     def end2(u):
         r = row_of(u)
@@ -430,15 +498,16 @@
     def adjoint_start(u):
         r = row_of(u)
         l1 = second(1, 0, 1, r).astype(BF16)
-        mv[3, pl.ds(r, CH), :] = l1
+        gg[3, u, :, 0:256] = l1
         gather_start(3, u)
         wide = l1.astype(F32) * 0.5
         l1f[0, pl.ds(r, CH), :] = wide[:, 0:128]
         l1f[1, pl.ds(r, CH), :] = wide[:, 128:256]
     units(adjoint_start)
 
-    for c in sends[0:4]:
+    for c in temps:
         c.wait_recv()
+    wait_x(0)
     rim_x(0, qs0, 8)
     rim_y(0, qs0, 3)
 
@@ -446,13 +515,13 @@
         return jnp.concatenate(
             [l1f[0, pl.ds(i, E, stride=E), :], l1f[1, pl.ds(i, E, stride=E), :]], axis=1
         )
+    gradient(qs0, weight0, 0, 2, True)
     gather_on(3)
-    gradient(qs0, weight0, 0, 2, True)
     pick(3, 0)
+    scatter_on(3)
     gradient(qs0, weight0, 2, 4, True)
     save = pltpu.make_async_copy(out, vg_hbm, ls.at[4])
     save.start()
-    scatter_on(3)
 
     def end3(u):
         r = row_of(u)
@@ -467,20 +536,29 @@
 
     for c in metas + sends:
         c.wait_send()
+
+    @pl.when(y == 3)
+    def _():
+        for f in range(4):
+            relay(f, 0).wait_send()
+
+    @pl.when(y == 0)
+    def _():
+        for f in range(4):
+            relay(f, 1).wait_send()
+
     for p in range(4):
         def drain(u, p=p):
-            for n in range(8):
+            for n in range(10):
                 xcopy(p, u, n).wait_send()
         units(drain)
     save.wait()
 
 
 def shards(template, target_image, velocity, operators, route, target_brick, operator_index):
-    index = jnp.stack(
-        [operator_index.reshape(16), route.reshape(16) * 8 + target_brick.reshape(16)]
-    )
     vmem = pl.BlockSpec(memory_space=pltpu.VMEM)
     hbm = pl.BlockSpec(memory_space=pl.ANY)
+    smem = pl.BlockSpec(memory_space=pltpu.SMEM)
     field = (E + 6, E + 16, 256)
     dma = pltpu.SemaphoreType.DMA
     vg, tg = pl.pallas_call(
@@ -489,21 +567,25 @@
             jax.ShapeDtypeStruct((3, E, E, 256), F32),
             jax.ShapeDtypeStruct((1024, 256), BF16),
         ),
-        in_specs=[pl.BlockSpec(memory_space=pltpu.SMEM), vmem, hbm, hbm, vmem],
+        in_specs=[smem, smem, smem, hbm, hbm, hbm, hbm],
         out_specs=(hbm, vmem),
         scratch_shapes=[
+            pltpu.VMEM((1024, 256), BF16),
+            pltpu.VMEM((3 * E * E, 64), BF16),
             pltpu.VMEM((2, 1024, 128), F32),
-            pltpu.VMEM((4, 1024, 256), BF16),
-            pltpu.VMEM((4, 4, 3, CH, 256), BF16),
+            pltpu.VMEM((4, 4, CH, 1024), BF16),
             pltpu.VMEM((4, 4, CH, 256), BF16),
             pltpu.VMEM((4, 4, 2, CH, 256), BF16),
             pltpu.VMEM((4, 4, 3, CH, 256), BF16),
-            pltpu.VMEM((4, 3, CH, 256), F32),
+            pltpu.VMEM((4, 2, CH, 256), F32),
             pltpu.VMEM((2, 2, 4, 4, 256, 256), BF16),
             pltpu.VMEM((2, 2, 2, 2, E, 128), BF16),
             pltpu.VMEM((2, 256, 256), BF16),
             pltpu.VMEM((2, 3, 256, E), BF16),
+            pltpu.VMEM((3, 16, 1024), F32),
+            pltpu.VMEM((1024, E), BF16),
             pltpu.VMEM((256, 256), BF16),
+            pltpu.VMEM((128, 256), BF16),
             pltpu.VMEM((E, 256), BF16),
             pltpu.VMEM((2, 256, 256), BF16),
             pltpu.VMEM((1024, 256), BF16),
@@ -516,30 +598,33 @@
             pltpu.VMEM((3, E, E, 256), F32),
             pltpu.VMEM((2, 1024, 128), F32),
             pltpu.VMEM((2, 1024, 128), F32),
-            pltpu.VMEM((4, 2, 96, 256), BF16),
+            pltpu.VMEM((4, 2, 2, 96, 256), BF16),
             pltpu.VMEM((3, 2, 96, 256), BF16),
             pltpu.VMEM((4, 2, E, 8, 256), F32),
             pltpu.VMEM((8, 256), jnp.int32),
             pltpu.VMEM((3, 8, 256), jnp.int32),
             pltpu.VMEM((3, 8, 256), jnp.int32),
-            dma((4, 4, 8)),
-            dma((4, 4, 8)),
+            dma((4, 4, 10)),
+            dma((4, 4, 10)),
             dma((4, 4)),
-            dma((4, 4)),
+            dma((4, 2)),
+            dma((4, 4, 2)),
             dma((6,)),
             dma((6,)),
-            dma((5,)),
+            dma((7,)),
         ],
         compiler_params=pltpu.CompilerParams(
             collective_id=0, has_side_effects=True, vmem_limit_bytes=62 << 20
         ),
         name="gradient",
     )(
-        index,
+        operator_index,
+        route.reshape(route.shape[:4]),
+        target_brick,
         template.reshape(1024, 256),
         target_image.reshape(1024, 256),
         velocity,
-        operators.reshape(64, 96, E),
+        operators.transpose(1, 2, 3, 0).reshape(3 * E * E, -1),
     )
     return vg, tg.reshape(E, E, 256)
 

time: 124 us -> 114 us (0.919)
  other arithmetic: 3.96 us -> 0 us
  local copies, waits for them, and re-layouts: 8.61 us -> 4.83 us
  Pallas kernels: 110 us -> 107 us
    unnamed x6 -> x4, local copies, waits for them, and re-layouts: 8.36 us -> 4.83 us
    pallas_call x1, Pallas kernels: 110 us -> 107 us  [shards(): pl.pallas_call(kernel, out_shape=(jax.ShapeDtypeStruct((3, E, E, 256), F3...]
    unnamed x2 -> x0, other arithmetic: 2.68 us -> none
where the time goes in v2:
time: 114 us; the launch traced here: 112 us
  Pallas kernels  107 us (94%)
  local copies, waits for them, and re-layouts  4.83 us (4%)
    pallas_call x1, Pallas kernels, shards(): pl.pallas_call(kernel, out_shape=(jax.ShapeDtypeStruct((3, E, E, 256), F3...  107 us
    unnamed x4, local copies, waits for them, and re-layouts  4.83 us

profile of v2, /device:TPU:2, one launch (start us, length us, event | category | flops | bytes accessed | tf_op | source)
XLA Modules:
  0.0 112.3 jit_solution(16592142926173418788)
XLA Ops:
  0.6 106.8 %gradient.1 = (f32[3,32,32,256]{3,2,1,0:T(8,128)}, bf16[1024,256]{1,0:T(8,128)(2,1)}) custom-call(s32[2,1,1,8]{3,2,1,0:T(1,128)} %opi_ref.1, s32[2,1,1,8]{3,2,1,0:T(1,128)} %bitcast.13, s32[2,1,1,8]{3,2,1,0:T(1,128)} %brick_ref.1, bf16[1024,256]{1,0:T(8,128)(2,1)} %bitcast.10, bf16[1024,256]{1,0:T(8,128)(2,1)} %bitcast.11, f32[3,32,32,256]{3,2,1,0:T(8,128)} %vel_hbm.1, ...), custom_call_target="tpu_custom_call" | custom-call | tf_op jit(solution)/shard_map/gradient/pallas_call | solution.py:564
  107.5 0.0 copy-start
  107.5 4.0 %copy.12 = f32[3,32,32,256]{3,2,1,0:T(8,128)} copy(f32[3,32,32,256]{3,2,1,0:T(8,128)} %get-tuple-element.8) | data formatting | bytes 6291456
  111.5 0.0 copy-done
  111.5 0.8 copy.13
Async XLA Ops:
  107.5 4.0 %copy-start = (bf16[1024,256]{1,0:T(8,128)(2,1)S(1)}, bf16[1024,256]{1,0:T(8,128)(2,1)}, u32[]{:S(2)}) copy-start(bf16[1024,256]{1,0:T(8,128)(2,1)} %get-tuple-element.5) | copy-start | bytes 1572868

commit v3 on v2

--- a/solution.py
+++ b/solution.py
@@ -26,7 +26,7 @@
 
 
 def kernel(
-    opi_ref, route_ref, brick_ref, tmpl_hbm, targ_hbm, vel_hbm, ops_hbm, vg_hbm, tg_ref,
+    opi_ref, route_ref, brick_ref, tmpl_hbm, targ_hbm, vel_hbm, ops_hbm, vg_hbm, half_ref, last_ref,
     tmpl, ops_ref,
     f1, gg, r3, r12, ps, pf, sel, lhs, wc, ost, chosen, fold, mask, mask4, tile, dz, targ,
     qs0, qs1, qd, qv0, qv1, v2, out, s1f, l1f, hx, hxs, hy, meta, mz, my,
@@ -166,12 +166,14 @@
                 store(i, j, res[:, 0:128])
                 store(i + 1, j, res[:, 128:256])
 
-    def first(t, k, tr, row0, value):
+    def first(t, k, tr, row0, value, into=None):
+        into = f1 if into is None else into
+
         def load(i, j):
             return value[i * E:(i + 1) * E, j * 128:(j + 1) * 128]
 
         def store(i, j, res):
-            f1[j, pl.ds(row0 + i * E, E), :] = res
+            into[j, pl.ds(row0 + i * E, E), :] = res.astype(into.dtype)
 
         contract(t, k, tr, load, store)
 
@@ -526,13 +528,11 @@
     def end3(u):
         r = row_of(u)
         back = arrived(3, u).astype(BF16)
-        first(0, 0, 1, r, mm(back, wc[0]).astype(BF16))
+        first(0, 0, 1, r, mm(back, wc[0]).astype(BF16), half_ref)
     units(end3)
 
-    def finish(u):
-        r = row_of(u)
-        tg_ref[pl.ds(r, CH), :] = second(0, 1, 1, r).astype(BF16)
-    units(finish)
+    for j in range(2):
+        last_ref[j] = lhs[0, 1, 1, j]
 
     for c in metas + sends:
         c.wait_send()
@@ -555,20 +555,57 @@
     save.wait()
 
 
+def finish(half_hbm, last_ref, vg_in, vg_out, tg_ref, half, wide, mask, held, ls):
+    load = pltpu.make_async_copy(half_hbm, half, ls.at[0])
+    load.start()
+    fetches = [pltpu.make_async_copy(vg_in.at[k], held.at[k], ls.at[1 + k]) for k in range(3)]
+    copies = [pltpu.make_async_copy(held.at[k], vg_out.at[k], ls.at[4 + k]) for k in range(3)]
+    for c in fetches:
+        c.start()
+    mask[...] = jnp.where(iota((128, 256), 0) // E == iota((128, 256), 1) % 128 // E, 1.0, 0.0).astype(BF16)
+    load.wait()
+
+    def widen(u, carry):
+        r = pl.multiple_of(u * CH, CH)
+        for j in range(2):
+            wide[j, pl.ds(r, CH), :] = half[j, pl.ds(r, CH), :].astype(F32)
+        return carry
+    lax.fori_loop(0, 4, widen, 0)
+
+    def body(u, carry):
+        r = pl.multiple_of(u * CH, CH)
+        for j in range(2):
+            for i in range(0, 8, 2):
+                pair = [wide[j, pl.ds(u * 8 + i + n, E, stride=E), :].astype(BF16) for n in range(2)]
+                big = jnp.concatenate([jnp.concatenate(pair, axis=1)] * 4, axis=0) * mask[...]
+                res = mm(last_ref[j], big).astype(BF16)
+                for n in range(2):
+                    tg_ref[pl.ds(r + (i + n) * E, E), j * 128:(j + 1) * 128] = res[:, n * 128:(n + 1) * 128]
+        return carry
+    lax.fori_loop(0, 2, body, 0)
+    for k in range(3):
+        fetches[k].wait()
+        copies[k].start()
+    lax.fori_loop(2, 4, body, 0)
+    for c in copies:
+        c.wait()
+
+
 def shards(template, target_image, velocity, operators, route, target_brick, operator_index):
     vmem = pl.BlockSpec(memory_space=pltpu.VMEM)
     hbm = pl.BlockSpec(memory_space=pl.ANY)
     smem = pl.BlockSpec(memory_space=pltpu.SMEM)
     field = (E + 6, E + 16, 256)
     dma = pltpu.SemaphoreType.DMA
-    vg, tg = pl.pallas_call(
+    part, half, last = pl.pallas_call(
         kernel,
         out_shape=(
             jax.ShapeDtypeStruct((3, E, E, 256), F32),
-            jax.ShapeDtypeStruct((1024, 256), BF16),
+            jax.ShapeDtypeStruct((2, 1024, 128), BF16),
+            jax.ShapeDtypeStruct((2, E, 128), BF16),
         ),
         in_specs=[smem, smem, smem, hbm, hbm, hbm, hbm],
-        out_specs=(hbm, vmem),
+        out_specs=(hbm, vmem, vmem),
         scratch_shapes=[
             pltpu.VMEM((1024, 256), BF16),
             pltpu.VMEM((3 * E * E, 64), BF16),
@@ -626,6 +663,24 @@
         velocity,
         operators.transpose(1, 2, 3, 0).reshape(3 * E * E, -1),
     )
+    vg, tg = pl.pallas_call(
+        finish,
+        out_shape=(
+            jax.ShapeDtypeStruct((3, E, E, 256), F32),
+            jax.ShapeDtypeStruct((1024, 256), BF16),
+        ),
+        in_specs=[hbm, vmem, hbm],
+        out_specs=(hbm, vmem),
+        scratch_shapes=[
+            pltpu.VMEM((2, 1024, 128), BF16),
+            pltpu.VMEM((2, 1024, 128), F32),
+            pltpu.VMEM((128, 256), BF16),
+            pltpu.VMEM((3, E, E, 256), F32),
+            dma((7,)),
+        ],
+        compiler_params=pltpu.CompilerParams(vmem_limit_bytes=62 << 20),
+        name="finish",
+    )(half, last, part)
     return vg, tg.reshape(E, E, 256)
 
 

time: 114 us -> 112 us (0.982)
  local copies, waits for them, and re-layouts: 4.83 us -> 0 us
  Pallas kernels: 107 us -> 111 us
    pallas_call x0 -> x1, Pallas kernels: none -> 4.93 us  [shards(): pl.pallas_call(finish, out_shape=(jax.ShapeDtypeStruct((3, E, E, 256), F3...]
    unnamed x4 -> x0, local copies, waits for them, and re-layouts: 4.83 us -> none
    pallas_call x1, Pallas kernels: 107 us -> 106 us  [shards(): pl.pallas_call(kernel, out_shape=(jax.ShapeDtypeStruct((3, E, E, 256), F3...]
where the time goes in v3:
time: 112 us; the launch traced here: 111 us
  Pallas kernels  111 us (99%)
    pallas_call x1, Pallas kernels, shards(): pl.pallas_call(kernel, out_shape=(jax.ShapeDtypeStruct((3, E, E, 256), F3...  106 us
    pallas_call x1, Pallas kernels, shards(): pl.pallas_call(finish, out_shape=(jax.ShapeDtypeStruct((3, E, E, 256), F3...  4.93 us

profile of v3, /device:TPU:2, one launch (start us, length us, event | category | flops | bytes accessed | tf_op | source)
XLA Modules:
  0.0 111.2 jit_solution(15099127895889733412)
XLA Ops:
  0.6 105.6 %gradient.1 = (f32[3,32,32,256]{3,2,1,0:T(8,128)}, bf16[2,1024,128]{2,1,0:T(8,128)(2,1)}, bf16[2,32,128]{2,1,0:T(8,128)(2,1)}) custom-call(s32[2,1,1,8]{3,2,1,0:T(1,128)} %opi_ref.1, s32[2,1,1,8]{3,2,1,0:T(1,128)} %bitcast.12, s32[2,1,1,8]{3,2,1,0:T(1,128)} %brick_ref.1, bf16[1024,256]{1,0:T(8,128)(2,1)} %bitcast.10, bf16[1024,256]{1,0:T(8,128)(2,1)} %bitcast.11, ...), custom_call_target="tpu_custom_call" | custom-call | tf_op jit(solution)/shard_map/gradient/pallas_call | solution.py:600
  106.2 4.9 %finish.1 = (f32[3,32,32,256]{3,2,1,0:T(8,128)}, bf16[1024,256]{1,0:T(8,128)(2,1)}) custom-call(bf16[2,1024,128]{2,1,0:T(8,128)(2,1)} %get-tuple-element.7.half_hbm, bf16[2,32,128]{2,1,0:T(8,128)(2,1)} %get-tuple-element.8.last_ref, f32[3,32,32,256]{3,2,1,0:T(8,128)} %get-tuple-element.9.vg_in), custom_call_target="tpu_custom_call" | custom-call | tf_op jit(solution)/shard_map/finish/pallas_call | solution.py:666
